TPU v7x, 32 devices: a whole 2x2x4 slice. The times are simulated.
32 devices in a mesh: ctx: 16 (over z, y, x), ch: 2 (over core).
Axes of the slice: x: 2, y: 2, z: 4, core: 2. Of those that a mesh axis runs over, the one named last changes fastest.
Arguments:
- grad_out: bfloat16 [12288, 4096], P('ctx', 'ch'), may hold values from -6 to 6
- block_input: bfloat16 [12288, 4096], P('ctx', 'ch'), may hold values from -40 to 40
- norm_gain: bfloat16 [4096], P('ch'), may hold values from 0.5 to 1.5
- queries: bfloat16 [12288, 4096], P('ctx', 'ch'), may hold values from -6 to 6
- keys: bfloat16 [12288, 4096], P('ctx', 'ch'), may hold values from -6 to 6
- values: bfloat16 [12288, 4096], P('ctx', 'ch'), may hold values from -6 to 6
- filters: bfloat16 [256, 128], P('ch'), may hold values from -0.5 to 0.5
- doc_starts: int32 [16, 4], P('ctx'), may hold values from 0 to 767, as said below
- in_weight: bfloat16 [4096, 3, 4096], P('ctx', None, 'ch'), may hold values from -0.09375 to 0.09375
- out_weight: bfloat16 [4096, 4096], P('ch', 'ctx'), may hold values from -0.09375 to 0.09375
Outputs:
- grad_input: bfloat16 [12288, 4096], P('ctx', 'ch')
Inputs may be any that keep to these rules, and one draw needn't show every extreme that they name: `doc_starts`: each row holds 4 distinct document starts of one slab as offsets within the slab, in ascending order; the first slab's first start is 0.
All inputs are finite; a program needn't handle non-finite values.
Results may differ from a plain program's by a relative error of at most 0.013.
Values may be sent and summed in bfloat16 or wider, within the bound.
No kernel may reach another device: no remote copies, remote signals or barrier semaphores. Data moves between devices by JAX's collectives and lax.ppermute only.
A program may use at most 192 MiB of HBM per device.

v0:
```python
import functools

import jax
import jax.numpy as jnp
from jax import lax
from jax.experimental import pallas as pl
from jax.experimental.pallas import tpu as pltpu
from jax.sharding import Mesh
from jax.sharding import PartitionSpec as P

LANES = 128
EPSILON = 1e-05
VMEM_BYTES = 52 * 1024 * 1024

BRIEF = pl.CostEstimate(flops=1024, bytes_accessed=1024, transcendentals=0)

SWAP = [(1, 2), (2, 1)]
CYCLE = [(0, 2), (1, 0), (2, 3), (3, 1)]
PAIR = [(0, 1), (1, 0)]


def fence(*blocks):
    return lax.optimization_barrier(blocks)


def params(parallel):
    return pltpu.CompilerParams(
        dimension_semantics=("arbitrary",) * parallel, vmem_limit_bytes=VMEM_BYTES
    )


def toeplitz_into(table_ref, base_ref, taps, count):
    for q in range(count):
        row = jnp.broadcast_to(base_ref[q : q + 1, :], (taps, 2 * taps))
        band = pltpu.roll(row, 0, 1, stride=1, stride_axis=0)
        table_ref[q * taps : (q + 1) * taps, :] = band.astype(table_ref.dtype)


def banded(table, keep, source, taps, count):
    table = table.reshape(count, taps, 2 * taps)
    masked = (table * keep[None]).reshape(count * taps, 2 * taps)
    wide = jnp.dot(masked, source, preferred_element_type=jnp.float32)
    width = source.shape[1]
    owner = lax.broadcasted_iota(jnp.int32, (taps, width), 1) // (width // count)
    total = wide[:taps]
    for q in range(1, count):
        total = jnp.where(owner == q, wide[q * taps : (q + 1) * taps], total)
    return total


def forward_kernel(
    taps, count, base_ref, last_ref, tail_ref, keys_ref, values_ref, mix_ref, q_ref, table_ref, source_ref,
):
    rows, width = keys_ref.shape
    parts = width // LANES
    toeplitz_into(table_ref, base_ref, taps, parts * count)
    source_ref[:taps, :] = tail_ref[...]
    source_ref[taps:, :] = (keys_ref[...].astype(jnp.float32) * values_ref[...].astype(jnp.float32)).astype(
        jnp.bfloat16
    )

    def tile(i, carry):
        row = pl.multiple_of(i * taps, taps)
        col = lax.broadcasted_iota(jnp.int32, (taps, 2 * taps), 1) + (i - 1) * taps
        keep = jnp.where(col >= last_ref[pl.ds(row, taps), :], 1.0, 0.0).astype(jnp.bfloat16)
        for p in range(parts):
            lanes = slice(p * LANES, (p + 1) * LANES)
            table = table_ref[p * count * taps : (p + 1) * count * taps, :]
            mixed = banded(table, keep, source_ref[pl.ds(row, 2 * taps), lanes], taps, count)
            at = (pl.ds(row, taps), lanes)
            q_ref[at] = (mix_ref[at] * mixed).astype(q_ref.dtype)
        return carry

    lax.fori_loop(0, rows // taps, tile, 0)


def backward_kernel(
    taps, count, base_ref, last_ref, head_ref, keys_ref, values_ref, queries_ref, mix_ref,
    k_ref, v_ref, table_ref, source_ref,
):
    rows, width = keys_ref.shape
    parts = width // LANES
    toeplitz_into(table_ref, base_ref, taps, parts * count)
    source_ref[:rows, :] = (mix_ref[...] * queries_ref[...].astype(jnp.float32)).astype(jnp.bfloat16)
    source_ref[rows:, :] = head_ref[...]

    def tile(i, carry):
        row = pl.multiple_of(i * taps, taps)
        at_row = lax.broadcasted_iota(jnp.int32, (taps, 2 * taps), 0) + i * taps
        keep = jnp.where(at_row >= last_ref[:, pl.ds(row, 2 * taps)], 1.0, 0.0).astype(jnp.bfloat16)
        for p in range(parts):
            lanes = slice(p * LANES, (p + 1) * LANES)
            table = table_ref[p * count * taps : (p + 1) * count * taps, :]
            conv = banded(table, keep, source_ref[pl.ds(row, 2 * taps), lanes], taps, count)
            at = (pl.ds(row, taps), lanes)
            k_ref[at] = (conv * values_ref[at].astype(jnp.float32)).astype(k_ref.dtype)
            v_ref[at] = (conv * keys_ref[at].astype(jnp.float32)).astype(v_ref.dtype)
        return carry

    lax.fori_loop(0, rows // taps, tile, 0)


def conv_call(kernel, name, base, last, edge, operands, outs, taps, per, width, start=0):
    rows = operands[0].shape[0]
    cols = min(width, 4 * LANES)
    count = cols // LANES * per
    skip = start // cols
    slab = pl.BlockSpec((rows, cols), lambda g: (0, g + skip))
    return pl.pallas_call(
        functools.partial(kernel, taps, per),
        grid=(width // cols,),
        in_specs=[
            pl.BlockSpec((count, 2 * taps), lambda g: (g + skip, 0)),
            pl.BlockSpec(last.shape, lambda g: (0, 0)),
            pl.BlockSpec((taps, cols), lambda g: (0, g + skip)),
        ]
        + [slab] * len(operands),
        out_specs=[pl.BlockSpec((rows, cols), lambda g: (0, g))] * outs,
        out_shape=[jax.ShapeDtypeStruct((rows, width), jnp.bfloat16)] * outs,
        scratch_shapes=[
            pltpu.VMEM((count * taps, 2 * taps), jnp.bfloat16),
            pltpu.VMEM((rows + taps, cols), jnp.bfloat16),
        ],
        compiler_params=params(1),
        cost_estimate=BRIEF,
        name=name,
    )(base, last, edge, *operands)


NT = (((1,), (1,)), ((), ()))


def mix_kernel(at_ref, *refs):
    lefts, own_ref, sib_ref, out_ref = refs[:-3], *refs[-3:]
    step = pl.program_id(1)
    both = None
    for n, left in enumerate(lefts):
        right = (own_ref, sib_ref)[n % 2][n // 2]
        part = lax.dot_general(left[...], right, NT, preferred_element_type=jnp.float32)
        both = part if both is None else both + part

    @pl.when(step == 0)
    def _():
        out_ref[...] = both

    @pl.when(step > 0)
    def _():
        out_ref[...] += both


def mix_matmul(at, grads, own, sib):
    rows = grads.shape[0]
    blocks, width, feats = own.shape
    cols = min(width, 1024)
    lefts = [
        pl.BlockSpec((rows, feats), lambda n, j, at, side=side, k=k: (0, at[side, 2 * j + k]))
        for k in range(2)
        for side in range(2)
    ]
    right = pl.BlockSpec((2, cols, feats), lambda n, j, at: (j, n, 0))
    return pl.pallas_call(
        mix_kernel,
        grid_spec=pltpu.PrefetchScalarGridSpec(
            num_scalar_prefetch=1,
            grid=(width // cols, blocks // 2),
            in_specs=lefts + [right, right],
            out_specs=pl.BlockSpec((rows, cols), lambda n, j, at: (0, n)),
        ),
        out_shape=jax.ShapeDtypeStruct((rows, width), jnp.float32),
        compiler_params=params(2),
        cost_estimate=BRIEF,
        name="mix_matmul",
    )(at, *[grads] * len(lefts), own, sib)


def project_kernel(places, blocks, *refs):
    half = pl.num_programs(0) // 2
    own, sib = refs[: len(places)], refs[len(places) : 2 * len(places)]
    weights, outs = refs[2 * len(places) : -2], refs[-2:]

    def into(grads, out_ref):
        for n in range(blocks):
            total = None
            for grad, (b, left) in zip(grads, places):
                right = weights[n][b, :, left : left + grad.shape[1]]
                part = lax.dot_general(grad[...], right, NT, preferred_element_type=jnp.float32)
                total = part if total is None else total + part
            out_ref[n] = total.astype(out_ref.dtype)

    @pl.when(pl.program_id(0) < half)
    def _():
        into(own, outs[0])

    @pl.when(pl.program_id(0) >= half)
    def _():
        into(sib, outs[1])


def project(own, sib, weights):
    blocks = len(weights)
    branches, feats, width = weights[0].shape
    rows = own[0][0].shape[0]
    places = [
        (b, sum(p.shape[1] for p in pieces[:at])) for b, pieces in enumerate(own) for at in range(len(pieces))
    ]
    own, sib = [p for pieces in own for p in pieces], [p for pieces in sib for p in pieces]
    half = 2
    step = rows // half

    def first(i):
        return jnp.minimum(i, half - 1)

    def second(i):
        return jnp.maximum(i - half, 0)

    out = jax.ShapeDtypeStruct((blocks, rows, feats), jnp.bfloat16)
    return pl.pallas_call(
        functools.partial(project_kernel, places, blocks),
        grid=(2 * half,),
        in_specs=[pl.BlockSpec((step, p.shape[1]), lambda i: (first(i), 0)) for p in own]
        + [pl.BlockSpec((step, p.shape[1]), lambda i: (second(i), 0)) for p in sib]
        + [
            pl.BlockSpec((branches, feats, width), lambda i: (0, 0, 0), pipeline_mode=pl.Buffered(1))
        ]
        * blocks,
        out_specs=[
            pl.BlockSpec((blocks, step, feats), lambda i: (0, first(i), 0)),
            pl.BlockSpec((blocks, step, feats), lambda i: (0, second(i), 0)),
        ],
        out_shape=[out, out],
        compiler_params=params(1),
        cost_estimate=BRIEF,
        name="project",
    )(*own, *sib, *weights)


def pick_kernel(at_ref, own_ref, sib_ref, input_ref, gain_ref, norm_ref, cross_ref):
    step = pl.program_id(0)
    ours = (lax.broadcasted_iota(jnp.int32, own_ref.shape[1:], 0) * 0 + at_ref[2, step]) == 1
    norm = jnp.where(ours, own_ref[0].astype(jnp.float32), sib_ref[0].astype(jnp.float32))
    norm_ref[...] = norm.astype(norm_ref.dtype)
    part = jnp.sum(
        gain_ref[...].astype(jnp.float32) * norm * input_ref[...].astype(jnp.float32),
        axis=1,
        keepdims=True,
    )

    @pl.when(step == 0)
    def _():
        cross_ref[...] = part

    @pl.when(step > 0)
    def _():
        cross_ref[...] += part


def pick(at, own, sib, block_input, gain):
    rows, width = block_input.shape
    feats = own.shape[2]
    return pl.pallas_call(
        pick_kernel,
        grid_spec=pltpu.PrefetchScalarGridSpec(
            num_scalar_prefetch=1,
            grid=(width // feats,),
            in_specs=[
                pl.BlockSpec((1, rows, feats), lambda j, at: (at[0, j], 0, 0)),
                pl.BlockSpec((1, rows, feats), lambda j, at: (at[1, j], 0, 0)),
                pl.BlockSpec((rows, feats), lambda j, at: (0, j)),
                pl.BlockSpec((1, feats), lambda j, at: (0, j)),
            ],
            out_specs=[
                pl.BlockSpec((rows, feats), lambda j, at: (0, j)),
                pl.BlockSpec((rows, 1), lambda j, at: (0, 0)),
            ],
        ),
        out_shape=[
            jax.ShapeDtypeStruct((rows, width), jnp.bfloat16),
            jax.ShapeDtypeStruct((rows, 1), jnp.float32),
        ],
        compiler_params=params(1),
        cost_estimate=BRIEF,
        name="pick",
    )(at, own, sib, block_input, gain)


def finish_kernel(features, groups, at_ref, *refs):
    input_ref, gain_ref, inverse_ref, grad_ref, out_ref, norm_ref = refs[2 * groups :]
    count, step, feats = norm_ref.shape[1:]
    c = at_ref[2, 0]
    for parity, blocks in ((c, refs[:groups]), (1 - c, refs[groups : 2 * groups])):
        first = 0
        for block in blocks:
            norm_ref[parity, first : first + block.shape[0]] = block[...]
            first += block.shape[0]

    cross = jnp.zeros((step, feats), jnp.float32)
    for n in range(count):
        for parity in range(2):
            block = at_ref[0, n] * 2 + parity
            left = pl.multiple_of(lax.rem(block, count) * feats, feats)
            half = lax.div(block, count)
            gain = gain_ref[half, :, pl.ds(left, feats)].astype(jnp.float32)
            source = input_ref[half, :, pl.ds(left, feats)].astype(jnp.float32)
            cross += gain * norm_ref[parity, n].astype(jnp.float32) * source
    inverse = inverse_ref[...]
    scale = inverse * inverse * inverse * jnp.sum(cross, axis=1, keepdims=True) / features
    for j in range(count):
        cols = slice(j * feats, (j + 1) * feats)
        block = c * count + j
        place = at_ref[1, lax.div(block, 2)]
        scaled = gain_ref[c, :, cols].astype(jnp.float32) * norm_ref[lax.rem(block, 2), place].astype(jnp.float32)
        result = grad_ref[:, cols].astype(jnp.float32) + inverse * scaled
        result -= input_ref[c, :, cols].astype(jnp.float32) * scale
        out_ref[:, cols] = result.astype(out_ref.dtype)


def finish(at, own, sib, inputs, gains, inverse, grad_out):
    rows, width = grad_out.shape
    count, feats = at.shape[1], own[0].shape[2]
    step = min(rows, 128)

    slab = pl.BlockSpec((step, width), lambda i, at: (i, 0))
    return pl.pallas_call(
        functools.partial(finish_kernel, 2 * width, len(own)),
        grid_spec=pltpu.PrefetchScalarGridSpec(
            num_scalar_prefetch=1,
            grid=(rows // step,),
            in_specs=[
                pl.BlockSpec((group.shape[0], step, feats), lambda i, at: (0, i, 0)) for group in (*own, *sib)
            ]
            + [
                pl.BlockSpec((2, step, width), lambda i, at: (0, i, 0)),
                pl.BlockSpec((2, 1, width), lambda i, at: (0, 0, 0)),
                pl.BlockSpec((step, 1), lambda i, at: (i, 0)),
                slab,
            ],
            out_specs=slab,
            scratch_shapes=[pltpu.VMEM((2, count, step, feats), jnp.bfloat16)],
        ),
        out_shape=jax.ShapeDtypeStruct((rows, width), jnp.bfloat16),
        compiler_params=params(1),
        cost_estimate=BRIEF,
        name="finish",
    )(at, *own, *sib, inputs, gains, inverse, grad_out)


def on_device(
    ring,
    n_chan,
    grad_out,
    block_input,
    norm_gain,
    queries,
    keys,
    values,
    filters,
    doc_starts,
    in_weight,
    out_weight,
):
    rows, width = grad_out.shape
    groups, taps = filters.shape
    feats, branches = in_weight.shape[:2]
    count = len(ring)
    per = LANES * groups // width
    features = feats * 2 * count
    o, x, h, c = (lax.axis_index(a) for a in ("o", "x", "h", "c"))
    order = jnp.array(ring, jnp.int32)
    place = jnp.array([ring.index(i) for i in range(count)], jnp.int32)
    position = place[o]
    far = count // 2
    forth = [(ring[i], ring[(i + 1) % count]) for i in range(count)]
    back = [(b, a) for a, b in forth]

    def exchanged(block):
        return lax.ppermute(block, ("x", "c"), SWAP)

    def swapped(block):
        return jnp.where(x == c, block, exchanged(block))

    def sibling(block):
        return lax.ppermute(block, "c", PAIR)

    def both_ways(up, down):
        return lax.ppermute(up, ("o",), forth), lax.ppermute(down, ("o",), back)

    def far_halves(up, down, axis):
        half = up.shape[axis] // 2
        return both_ways(
            lax.slice_in_dim(up, 0, half, axis=axis),
            lax.slice_in_dim(down, half, 2 * half, axis=axis),
        )

    def neighbour(block, distance):
        route = []
        for i in range(count):
            for core in range(2):
                source = i * 2 + core + distance
                if 0 <= source < 2 * count:
                    route += [(source * 2 + side, (i * 2 + side) * 2 + core) for side in range(2)]
        return lax.ppermute(block, ("o", "x", "c"), route)

    starts = swapped(doc_starts)[0]
    prior = neighbour(doc_starts, -1)[0, -1]
    following = neighbour(doc_starts, 1)[0]
    tail = (keys[rows - taps :].astype(jnp.float32) * values[rows - taps :].astype(jnp.float32)).astype(
        jnp.bfloat16
    )
    taps32 = swapped(filters).astype(jnp.float32)
    out_w = swapped(out_weight)
    in_w = jnp.swapaxes(in_weight, 0, 1)
    out_w, in_w, grad_out, taps32, starts, prior, following, tail = fence(
        out_w, in_w, grad_out, taps32, starts, prior, following, tail
    )

    in_recv = exchanged(in_w)
    sib_in, sib_gain = sibling(block_input), sibling(norm_gain)
    blocks = [out_w]
    up = down = out_w
    for s in range(1, far):
        up, down = both_ways(up, down)
        if s == far - 2:
            up, down, in_recv, in_w, grad_out, queries, sib_in, sib_gain = fence(
                up, down, in_recv, in_w, grad_out, queries, sib_in, sib_gain
            )
        blocks += [up, down]
    in_w = jnp.where(x == c, in_w, in_recv)
    half_recv = exchanged(grad_out)
    first_q = exchanged(queries[:taps])
    blocks.append(jnp.concatenate(far_halves(up, down, 0), axis=0))
    own_out = jnp.stack(blocks)
    def in_order(own, sib):
        return jnp.where(c == 0, jnp.stack([own, sib]), jnp.stack([sib, own]))

    inputs, gains = in_order(block_input, sib_in), in_order(norm_gain, sib_gain)[:, None]
    square_sum = jnp.sum(jnp.square(inputs.astype(jnp.float32)), axis=(0, 2))[:, None]
    if n_chan > 1:
        square_sum = lax.psum(square_sum, "h")
    inverse = lax.rsqrt(square_sum / features + EPSILON)
    distances = [0] + [d for s in range(1, far) for d in (-s, s)] + [far]
    sources = order[(position + jnp.array(distances, jnp.int32)) % count]
    wide = width // feats

    def column(parity):
        block = sources * 2 + parity
        owner = block // wide
        side = jnp.where(owner % 2 == x, 0, 1)
        return side * (n_chan * wide) + (owner // 2) * wide + block % wide

    columns = jnp.stack([column(c), column(1 - c)])
    slabs = 2 * count
    backward = [(i + 1, i) for i in range(slabs - 1)]
    positions = jnp.arange(rows, dtype=jnp.int32)

    def last_of(own, before):
        own = jnp.where(own[None, :] <= positions[:, None], own[None, :], -rows)
        return jnp.maximum(jnp.max(own, axis=1), before - rows)

    last_start = last_of(starts, prior)
    padded_last = jnp.concatenate([last_start, last_of(following, starts[-1])[:taps] + rows])[None]
    edge = jnp.zeros((groups, taps), jnp.float32)
    base_back = jnp.concatenate([taps32, edge], axis=1)
    base_fore = jnp.concatenate([edge[:, :1], taps32[:, ::-1], edge[:, 1:]], axis=1)
    (
        own_out, in_w, half_recv, first_q, grad_out, queries, inverse, inputs, gains, padded_last, last_col,
        base_back, base_fore, columns,
    ) = fence(
        own_out, in_w, half_recv, first_q, grad_out, queries, inverse, inputs, gains, padded_last,
        last_start[:, None], base_back, base_fore, columns,
    )

    ahead, behind = {0: in_w}, {0: in_w}
    ahead[1], behind[1] = both_ways(in_w, in_w)
    sib_out = sibling(own_out)
    grad_other = lax.ppermute(grad_out, ("x", "c"), CYCLE)
    grad_other, keys, tail = fence(grad_other, keys, tail)
    k_recv = exchanged(keys)
    tail = neighbour(tail, -1)
    grad_half = jnp.where(x == c, grad_out, half_recv)
    if n_chan > 1:
        grad_half = lax.all_gather(grad_half, "h", axis=1, tiled=True)
        grad_other = lax.all_gather(grad_other, "h", axis=1, tiled=True)
    grads = jnp.concatenate([grad_half, grad_other], axis=1)
    mix_grad = mix_matmul(columns, grads, own_out, sib_out)
    ahead[1], behind[1], mix_grad, k_recv, keys, values = fence(
        ahead[1], behind[1], mix_grad, k_recv, keys, values
    )

    ahead[2], behind[2] = both_ways(ahead[1], behind[1])
    v_recv = exchanged(values)
    head = mix_grad[:taps] * jnp.where(x == c, queries[:taps], first_q).astype(jnp.float32)
    head = lax.ppermute(head.astype(jnp.bfloat16), ("o", "c"), backward)
    own_k = jnp.where(x == c, keys, k_recv)
    v_recv, values, own_k, queries, tail = fence(v_recv, values, own_k, queries, tail)
    q_recv = exchanged(queries)
    own_v = jnp.where(x == c, values, v_recv)
    middle = width // 2

    def halves(kernel, name, *operands, outs):
        return [
            conv_call(kernel, name, *operands, outs, taps, per, middle, start) for start in (0, middle)
        ]

    (q_left,), (q_right,) = halves(
        forward_kernel, "forward_conv", base_fore, last_col, tail, [own_k, own_v, mix_grad], outs=1
    )
    sib_left = sibling(q_left)
    ahead[2], behind[2], q_left, q_right, sib_left, head, q_recv, queries = fence(
        ahead[2], behind[2], q_left, q_right, sib_left, head, q_recv, queries
    )

    upper, lower = slice(0, feats // 2), slice(feats // 2, feats)
    early = both_ways(ahead[2][:, upper], behind[2][:, upper])
    late = both_ways(ahead[2][:, lower], behind[2][:, lower])
    own_q = jnp.where(x == c, queries, q_recv)
    grads = []
    for start in (0, middle):
        k_half, v_half = conv_call(
            backward_kernel, "backward_conv", base_back, padded_last, head, [own_k, own_v, own_q, mix_grad], 2,
            taps, per, middle, start,
        )
        if start > 0:
            *early, k_half, v_half = fence(*early, k_half, v_half)
        grads.append((k_half, v_half))
    own_grads = [[q_left, q_right]] + [[half[b] for half in grads] for b in range(2)]
    sib_grads = [[sib_left, sibling(q_right)]] + [[sibling(half[b]) for half in grads] for b in range(2)]

    def partial_sums(weights):
        ours, theirs = project(own_grads, sib_grads, weights)
        return jnp.where(c == x, ours, theirs), jnp.where(c == x, theirs, ours)

    def summed(keep, received):
        return (keep.astype(jnp.float32) + received.astype(jnp.float32)).astype(jnp.bfloat16)

    def over_x(block):
        return lax.ppermute(block, "x", PAIR)

    keep, send = partial_sums([in_w, ahead[1], behind[1]])
    *early, late_up, late_down, keep, send = fence(*early, *late, keep, send)
    ahead[3] = jnp.concatenate([early[0], late_up], axis=1)
    behind[3] = jnp.concatenate([early[1], late_down], axis=1)
    norms = []
    for s in range(4, far + 1):
        if s < far:
            up, down = both_ways(ahead[s - 1], behind[s - 1])
        else:
            up, down = far_halves(ahead[s - 1], behind[s - 1], 1)
        arrived = [(keep, over_x(send))]
        if s == 4:
            keep, send = partial_sums([ahead[2], behind[2]])
            keep, send, last_tail = fence(keep, send, own_grads[2][1])
            own_grads[2][1] = last_tail
            arrived.append((keep, over_x(send)))
        keep, send = partial_sums([ahead[s - 1], behind[s - 1]])
        flat = [block for pair in arrived for block in pair]
        up, down, keep, send, *flat = fence(up, down, keep, send, *flat)
        norms += [summed(*flat[i : i + 2]) for i in range(0, len(flat), 2)]
        ahead[s], behind[s] = up, down
    far_keep, far_send = partial_sums([jnp.concatenate([up, down], axis=1)])
    norms += [summed(keep, over_x(send)), summed(far_keep, over_x(far_send))]
    slot = jnp.zeros((count,), jnp.int32).at[sources].set(jnp.arange(count, dtype=jnp.int32))
    if n_chan == 1:
        others = [sibling(n) for n in norms]
        at = jnp.stack([sources, slot, jnp.full((count,), c, jnp.int32)])
        return finish(at, norms, others, inputs, gains, inverse, grad_out)

    norm = lax.psum_scatter(
        jnp.take(jnp.concatenate(norms, axis=0), slot, axis=0), "h", scatter_dimension=0, tiled=True
    )
    other = sibling(norm)
    mine = (h * 2 + c) * wide + jnp.arange(wide, dtype=jnp.int32)
    slots = mine // 2 - h * (count // n_chan)
    at = jnp.stack([slots, slots, (mine % 2 == c).astype(jnp.int32)])
    norm_grad, cross = pick(at, norm, other, block_input, norm_gain[None])
    cross_sum = lax.psum(cross, ("h", "c"))
    scaled = norm_gain.astype(jnp.float32)[None, :] * norm_grad.astype(jnp.float32)
    result = (
        grad_out.astype(jnp.float32)
        + inverse * scaled
        - block_input.astype(jnp.float32) * (inverse * inverse * inverse) * cross_sum / features
    )
    return result.astype(jnp.bfloat16)


def solution(mesh):
    outer, n_chan = mesh.shape["ctx"] // 2, mesh.shape["ch"] // 2
    split = Mesh(mesh.devices.reshape(outer, 2, n_chan, 2), ("o", "x", "h", "c"))
    ring = list(range(0, outer, 2)) + list(range(outer - 1, 0, -2))
    tok, chan = ("o", "x"), ("h", "c")
    placed = (
        P(tok, chan),
        P(tok, chan),
        P(chan),
        P(tok, chan),
        P(tok, chan),
        P(tok, chan),
        P(chan, None),
        P(tok, None),
        P(tok, None, chan),
        P(chan, tok),
    )
    return jax.shard_map(
        functools.partial(on_device, ring, n_chan),
        mesh=split,
        in_specs=placed,
        out_specs=P(tok, chan),
        check_vma=False,
    )
```

profile of v0, /device:TPU:0, one launch (start us, length us, event | category | flops | bytes accessed | tf_op | source)
XLA Modules:
  0.0 459.0 jit_solution(2539989221072884280)
XLA Ops:
  2.8 7.4 %collective-permute-start.3 = (s32[1,4]{1,0:T(1,128)}, s32[1,4]{1,0:T(1,128)S(1)}, u32[]{:S(2)}, u32[]{:S(2)}) collective-permute-start(s32[1,4]{1,0:T(1,128)} %param.20), channel_id=1, source_target_pairs={{0,1},{1,3},{2,4},{3,6},{4,5},{5,7},{6,8},{7,10},{8,9},{9,11},{10,... | collective-permute-start | bytes 56 | tf_op jit(solution)/shard_map/ppermute | solution.py:401
  17.6 4.0 collective-permute-start.10
  33.7 20.1 %collective-permute-done.6 = bf16[2048,256]{1,0:T(8,128)(2,1)S(1)} collective-permute-done((bf16[2048,256]{1,0:T(8,128)(2,1)S(1)}, bf16[2048,256]{1,0:T(8,128)(2,1)S(1)}, u32[]{:S(2)}, u32[]{:S(2)}) %collective-permute-start.6) | collective-permute-done | bytes 1048608 | tf_op jit(solution)/shard_map/ppermute | solution.py:385
  57.9 20.5 %collective-permute-done.8 = bf16[2048,256]{1,0:T(8,128)(2,1)S(1)} collective-permute-done((bf16[2048,256]{1,0:T(8,128)(2,1)S(1)}, bf16[2048,256]{1,0:T(8,128)(2,1)S(1)}, u32[]{:S(2)}, u32[]{:S(2)}) %collective-permute-start.8) | collective-permute-done | bytes 1048608 | tf_op jit(solution)/shard_map/ppermute | solution.py:385
  86.5 8.5 %multiply_reduce_fusion = (f32[768]{0:T(1024)S(1)}, bf16[2,768,2048]{2,1,0:T(8,128)(2,1)}) fusion(bf16[1,768,2048]{2,1,0:T(8,128)(2,1)S(1)} %bitcast.37, bf16[1,768,2048]{2,1,0:T(8,128)(2,1)} %bitcast.18, pred[]{:T(512)S(6)} %eq.56), kind=kLoop, calls=%fused_computation.2 | loop fusion | flops 18873600 | bytes 12585985 | tf_op jit(solution)/shard_map/reduce_sum | solution.py:436
  97.4 9.8 %collective-permute-done.12 = bf16[2048,256]{1,0:T(8,128)(2,1)S(1)} collective-permute-done((bf16[2048,256]{1,0:T(8,128)(2,1)S(1)}, bf16[2048,256]{1,0:T(8,128)(2,1)S(1)}, u32[]{:S(2)}, u32[]{:S(2)}) %collective-permute-start.12) | collective-permute-done | bytes 1048608 | tf_op jit(solution)/shard_map/ppermute | solution.py:385
  111.7 9.9 %collective-permute-done.14 = bf16[1024,256]{1,0:T(8,128)(2,1)S(1)} collective-permute-done((bf16[1024,256]{1,0:T(8,128)(2,1)S(1)}, bf16[1024,256]{1,0:T(8,128)(2,1)S(1)}, u32[]{:S(2)}, u32[]{:S(2)}) %collective-permute-start.14) | collective-permute-done | bytes 524320 | tf_op jit(solution)/shard_map/ppermute | solution.py:385
  127.0 32.8 %collective-permute-done.20 = bf16[768,2048]{1,0:T(8,128)(2,1)} collective-permute-done((bf16[768,2048]{1,0:T(8,128)(2,1)S(1)}, bf16[768,2048]{1,0:T(8,128)(2,1)}, u32[]{:S(2)}, u32[]{:S(2)}) %collective-permute-start.20) | collective-permute-done | bytes 3145760 | tf_op jit(solution)/shard_map/ppermute | solution.py:475
  162.4 5.3 %pad_maximum_fusion.refs_0_.refs_1_.refs_2_.refs_3_ = bf16[768,4096]{1,0:T(8,128)(2,1)} fusion(bf16[768,2048]{1,0:T(8,128)(2,1)} %collective-permute-done.20, bf16[768,2048]{1,0:T(8,128)(2,1)S(1)} %broadcast_select_fusion.3), kind=kLoop, calls=%fused_computation.4 | loop fusion | flops 12582912 | bytes 12582912 | tf_op jit(solution)/shard_map/concatenate | solution.py:483
  167.7 23.3 %mix_matmul.1.mix_ref = f32[768,2048]{1,0:T(8,128)} custom-call(s32[2,8]{1,0:T(2,128)S(1)} %pad_add_fusion.2.at_ref, bf16[768,4096]{1,0:T(8,128)(2,1)} %pad_maximum_fusion.refs_0_.refs_1_.refs_2_.refs_3_, bf16[768,4096]{1,0:T(8,128)(2,1)} %pad_maximum_fusion.refs_0_.refs_1_.refs_2_.refs_3_, ...), custom_call_target="tpu_custom_call" | custom-call | flops 1024 | bytes 1024 | tf_op jit(solution)/shard_map/mix_matmul/pallas_call | solution.py:161
  197.6 7.4 %collective-permute-start.26 = (bf16[128,2048]{1,0:T(8,128)(2,1)S(1)}, bf16[128,2048]{1,0:T(8,128)(2,1)S(1)}, u32[]{:S(2)}, u32[]{:S(2)}) collective-permute-start(bf16[128,2048]{1,0:T(8,128)(2,1)S(1)} %copy-done.9), channel_id=1, source_target_pairs={{0,1},{1,3},{2,4},{3,6},{4,5},{5,7},{6,8},{7,10},{8,9},{9,11},{10,... | collective-permute-start | bytes 1572872 | tf_op jit(solution)/shard_map/ppermute | solution.py:401
  215.4 14.0 %forward_conv.2.refs_0_ = bf16[768,1024]{1,0:T(8,128)(2,1)} custom-call(f32[128,256]{1,0:T(8,128)S(1)} %maximum_maximum_fusion.base_ref, s32[768,1]{1,0:T(8,128)S(1)} %copy.17.last_ref, bf16[128,2048]{1,0:T(8,128)(2,1)S(1)} %collective-permute-done.26.tail_ref, bf16[768,2048]{1,0:T(8,128)(2,1)} %broadcast_select_fusion.2.keys_ref, ...), custom_call_target="tpu_custom_call" | custom-call | flops 1024 | bytes 1024 | tf_op jit(solution)/shard_map/forward_conv/pallas_call | solution.py:109
  229.5 34.2 %collective-permute-start.27 = (bf16[768,1024]{1,0:T(8,128)(2,1)}, bf16[768,1024]{1,0:T(8,128)(2,1)S(1)}, u32[]{:S(2)}, u32[]{:S(2)}) collective-permute-start(bf16[768,1024]{1,0:T(8,128)(2,1)} %forward_conv.2.refs_0_), channel_id=1, source_target_pairs={{0,1},{1,0},{2,3},{3,2},{4,5},{5,4},{6,7},{7,6},{8,9},{9,8},{10,11... | collective-permute-start | bytes 4718600 | tf_op jit(solution)/shard_map/ppermute | solution.py:382
  266.7 14.0 %forward_conv.3.refs_1_ = bf16[768,1024]{1,0:T(8,128)(2,1)} custom-call(f32[128,256]{1,0:T(8,128)S(1)} %maximum_maximum_fusion.base_ref, s32[768,1]{1,0:T(8,128)S(1)} %copy.17.last_ref, bf16[128,2048]{1,0:T(8,128)(2,1)S(1)} %collective-permute-done.26.tail_ref, bf16[768,2048]{1,0:T(8,128)(2,1)} %broadcast_select_fusion.2.keys_ref, ...), custom_call_target="tpu_custom_call" | custom-call | flops 1024 | bytes 1024 | tf_op jit(solution)/shard_map/forward_conv/pallas_call | solution.py:109
  280.7 5.1 %collective-permute-done.24.refs_13_ = bf16[3,256,2048]{2,1,0:T(8,128)(2,1)} collective-permute-done((bf16[3,256,2048]{2,1,0:T(8,128)(2,1)}, bf16[3,256,2048]{2,1,0:T(8,128)(2,1)}, u32[]{:S(2)}, u32[]{:S(2)}) %collective-permute-start.24) | collective-permute-done | bytes 3145760 | tf_op jit(solution)/shard_map/ppermute | solution.py:385
  299.8 13.9 %backward_conv.3 = (bf16[768,1024]{1,0:T(8,128)(2,1)}, bf16[768,1024]{1,0:T(8,128)(2,1)}) custom-call(f32[128,256]{1,0:T(8,128)S(1)} %concatenate.40.base_ref, s32[1,896]{1,0:T(1,128)S(1)} %broadcast_in_dim.39.last_ref, bf16[128,2048]{1,0:T(8,128)(2,1)S(1)} %collective-permute-done.28.head_ref, bf16[768,2048]{1,0:T(8,128)(2,1)} %broadcast_select_fusion.2.keys_ref, ...), custom_call_target="tpu_custom_call" | custom-call | flops 1024 | bytes 1024 | tf_op jit(solution)/shard_map/backward_conv/pallas_call | solution.py:109
  313.7 14.0 %backward_conv.2 = (bf16[768,1024]{1,0:T(8,128)(2,1)}, bf16[768,1024]{1,0:T(8,128)(2,1)}) custom-call(f32[128,256]{1,0:T(8,128)S(1)} %concatenate.40.base_ref, s32[1,896]{1,0:T(1,128)S(1)} %broadcast_in_dim.39.last_ref, bf16[128,2048]{1,0:T(8,128)(2,1)S(1)} %collective-permute-done.28.head_ref, bf16[768,2048]{1,0:T(8,128)(2,1)} %broadcast_select_fusion.2.keys_ref, ...), custom_call_target="tpu_custom_call" | custom-call | flops 1024 | bytes 1024 | tf_op jit(solution)/shard_map/backward_conv/pallas_call | solution.py:109
  335.9 23.7 %project.4 = (bf16[3,768,256]{2,1,0:T(8,128)(2,1)S(1)}, bf16[3,768,256]{2,1,0:T(8,128)(2,1)}) custom-call(bf16[768,1024]{1,0:T(8,128)(2,1)} %forward_conv.2.refs_0_, bf16[768,1024]{1,0:T(8,128)(2,1)} %forward_conv.3.refs_1_, bf16[768,1024]{1,0:T(8,128)(2,1)} %get-tuple-element.142.refs_2_, bf16[768,1024]{1,0:T(8,128)(2,1)} %get-tuple-element.143.refs_3_, ...), custom_call_target="tpu_custom_call" | custom-call | flops 1024 | bytes 1024 | tf_op jit(solution)/shard_map/project/pallas_call | solution.py:217
  361.1 6.5 %collective-permute-done.32 = bf16[3,128,2048]{2,1,0:T(8,128)(2,1)} collective-permute-done((bf16[3,128,2048]{2,1,0:T(8,128)(2,1)}, bf16[3,128,2048]{2,1,0:T(8,128)(2,1)}, u32[]{:S(2)}, u32[]{:S(2)}) %collective-permute-start.32) | collective-permute-done | bytes 1572896 | tf_op jit(solution)/shard_map/ppermute | solution.py:385
  372.6 17.2 %project.5 = (bf16[2,768,256]{2,1,0:T(8,128)(2,1)S(1)}, bf16[2,768,256]{2,1,0:T(8,128)(2,1)S(1)}) custom-call(bf16[768,1024]{1,0:T(8,128)(2,1)} %forward_conv.2.refs_0_, bf16[768,1024]{1,0:T(8,128)(2,1)} %forward_conv.3.refs_1_, bf16[768,1024]{1,0:T(8,128)(2,1)} %get-tuple-element.142.refs_2_, bf16[768,1024]{1,0:T(8,128)(2,1)} %get-tuple-element.143.refs_3_, ...), custom_call_target="tpu_custom_call" | custom-call | flops 1024 | bytes 1024 | tf_op jit(solution)/shard_map/project/pallas_call | solution.py:217
  399.0 17.2 %project.6 = (bf16[2,768,256]{2,1,0:T(8,128)(2,1)S(1)}, bf16[2,768,256]{2,1,0:T(8,128)(2,1)S(1)}) custom-call(bf16[768,1024]{1,0:T(8,128)(2,1)} %forward_conv.2.refs_0_, bf16[768,1024]{1,0:T(8,128)(2,1)} %forward_conv.3.refs_1_, bf16[768,1024]{1,0:T(8,128)(2,1)} %get-tuple-element.142.refs_2_, bf16[768,1024]{1,0:T(8,128)(2,1)} %get-tuple-element.143.refs_3_, ...), custom_call_target="tpu_custom_call" | custom-call | flops 1024 | bytes 1024 | tf_op jit(solution)/shard_map/project/pallas_call | solution.py:217
  421.2 12.6 %project.7 = (bf16[1,768,256]{2,1,0:T(8,128)(2,1)S(1)}, bf16[1,768,256]{2,1,0:T(8,128)(2,1)S(1)}) custom-call(bf16[768,1024]{1,0:T(8,128)(2,1)} %forward_conv.2.refs_0_, bf16[768,1024]{1,0:T(8,128)(2,1)} %forward_conv.3.refs_1_, bf16[768,1024]{1,0:T(8,128)(2,1)} %get-tuple-element.142.refs_2_, bf16[768,1024]{1,0:T(8,128)(2,1)} %get-tuple-element.143.refs_3_, ...), custom_call_target="tpu_custom_call" | custom-call | flops 1024 | bytes 1024 | tf_op jit(solution)/shard_map/project/pallas_call | solution.py:217
  439.2 6.9 %collective-permute-done.44 = bf16[1,768,256]{2,1,0:T(8,128)(2,1)S(1)} collective-permute-done((bf16[1,768,256]{2,1,0:T(8,128)(2,1)S(1)}, bf16[1,768,256]{2,1,0:T(8,128)(2,1)S(1)}, u32[]{:S(2)}, u32[]{:S(2)}) %collective-permute-start.44) | collective-permute-done | bytes 393248 | tf_op jit(solution)/shard_map/ppermute | solution.py:536
  448.0 10.5 %finish.1 = bf16[768,2048]{1,0:T(8,128)(2,1)} custom-call(s32[3,8]{1,0:T(4,128)S(1)} %pad_add_fusion.1.at_ref, bf16[3,768,256]{2,1,0:T(8,128)(2,1)} %copy-done.5, bf16[2,768,256]{2,1,0:T(8,128)(2,1)S(1)} %add_convert_fusion.2.refs_1_, bf16[2,768,256]{2,1,0:T(8,128)(2,1)} %add_convert_fusion.1.refs_2_, bf16[1,768,256]{2,1,0:T(8,128)(2,1)S(1)} %add_convert_fusion.3.refs_3_, ...), custom_call_target="tpu_custom_call" | custom-call | flops 1024 | bytes 1024 | tf_op jit(solution)/shard_map/finish/pallas_call | solution.py:323
  (181 shorter events, 117.7 us)
Async XLA Ops:
  10.3 47.7 %collective-permute-start.11 = (bf16[2048]{0:T(1024)(128)(2,1)}, bf16[2048]{0:T(1024)(128)(2,1)S(1)}, u32[]{:S(2)}, u32[]{:S(2)}) collective-permute-start(bf16[2048]{0:T(1024)(128)(2,1)} %param.15), channel_id=1, source_target_pairs={{0,1},{1,0},{2,3},{3,2},{4,5},{5,4},{6,7},{7,6},{8,9},{9,8},{10,11... | collective-permute-start | bytes 12296 | tf_op jit(solution)/shard_map/ppermute | solution.py:382
  17.6 62.1 %collective-permute-start.10 = (bf16[768,2048]{1,0:T(8,128)(2,1)}, bf16[768,2048]{1,0:T(8,128)(2,1)}, u32[]{:S(2)}, u32[]{:S(2)}) collective-permute-start(bf16[768,2048]{1,0:T(8,128)(2,1)} %param.14), channel_id=1, source_target_pairs={{0,1},{1,0},{2,3},{3,2},{4,5},{5,4},{6,7},{7,6},{8,9},{9,8},{10,11... | collective-permute-start | bytes 9437192 | tf_op jit(solution)/shard_map/ppermute | solution.py:382
  24.4 55.2 %collective-permute-start.9 = (bf16[3,256,2048]{2,1,0:T(8,128)(2,1)}, bf16[3,256,2048]{2,1,0:T(8,128)(2,1)}, u32[]{:S(2)}, u32[]{:S(2)}) collective-permute-start(bf16[3,256,2048]{2,1,0:T(8,128)(2,1)} %bitcast.5), channel_id=1, source_target_pairs={{1,2},{2,1},{5,6},{6,5},{9,10},{10,9},{13,14},{14,13},{17,18},{18,... | collective-permute-start | bytes 9437192 | tf_op jit(solution)/shard_map/ppermute | solution.py:376
  80.7 42.3 %collective-permute-start.17 = (bf16[128,2048]{1,0:T(8,128)(2,1)S(1)}, bf16[128,2048]{1,0:T(8,128)(2,1)S(1)}, u32[]{:S(2)}, u32[]{:S(2)}) collective-permute-start(bf16[128,2048]{1,0:T(8,128)(2,1)S(1)} %slice.53), channel_id=1, source_target_pairs={{1,2},{2,1},{5,6},{6,5},{9,10},{10,9},{13,14},{14,13},{17,18},{18,... | collective-permute-start | bytes 1572872 | tf_op jit(solution)/shard_map/ppermute | solution.py:376
  83.5 39.5 %collective-permute-start.16 = (bf16[768,2048]{1,0:T(8,128)(2,1)S(1)}, bf16[768,2048]{1,0:T(8,128)(2,1)S(1)}, u32[]{:S(2)}, u32[]{:S(2)}) collective-permute-start(bf16[768,2048]{1,0:T(8,128)(2,1)S(1)} %copy-done.4), channel_id=1, source_target_pairs={{1,2},{2,1},{5,6},{6,5},{9,10},{10,9},{13,14},{14,13},{17,18},{18,... | collective-permute-start | bytes 9437192 | tf_op jit(solution)/shard_map/ppermute | solution.py:376
  123.0 44.7 %collective-permute-start.21 = (bf16[8,2048,256]{2,1,0:T(8,128)(2,1)}, bf16[8,2048,256]{2,1,0:T(8,128)(2,1)}, u32[]{:S(2)}, u32[]{:S(2)}) collective-permute-start(bf16[8,2048,256]{2,1,0:T(8,128)(2,1)} %fusion.refs_4_), channel_id=1, source_target_pairs={{0,1},{1,0},{2,3},{3,2},{4,5},{5,4},{6,7},{7,6},{8,9},{9,8},{10,11... | collective-permute-start | bytes 25165832 | tf_op jit(solution)/shard_map/ppermute | solution.py:382
  123.3 36.4 %collective-permute-start.20 = (bf16[768,2048]{1,0:T(8,128)(2,1)S(1)}, bf16[768,2048]{1,0:T(8,128)(2,1)}, u32[]{:S(2)}, u32[]{:S(2)}) collective-permute-start(bf16[768,2048]{1,0:T(8,128)(2,1)S(1)} %copy-done.4), channel_id=1, source_target_pairs={{0,2},{1,0},{2,3},{3,1},{4,6},{5,4},{6,7},{7,5},{8,10},{9,8},{10,1... | collective-permute-start | bytes 9437192 | tf_op jit(solution)/shard_map/ppermute | solution.py:475
  124.9 69.0 %collective-permute-start.19 = (bf16[3,256,2048]{2,1,0:T(8,128)(2,1)S(1)}, bf16[3,256,2048]{2,1,0:T(8,128)(2,1)}, u32[]{:S(2)}, u32[]{:S(2)}) collective-permute-start(bf16[3,256,2048]{2,1,0:T(8,128)(2,1)S(1)} %broadcast_select_fusion.4.refs_12_), channel_id=1, source_target_pairs={{8,0},{16,8},{24,16},{28,24},{20,28},{12,20},{4,12},{0,4},{9,1},{1... | collective-permute-start | bytes 9437192 | tf_op jit(solution)/shard_map/ppermute | solution.py:385
  126.5 68.7 %collective-permute-start.18 = (bf16[3,256,2048]{2,1,0:T(8,128)(2,1)S(1)}, bf16[3,256,2048]{2,1,0:T(8,128)(2,1)}, u32[]{:S(2)}, u32[]{:S(2)}) collective-permute-start(bf16[3,256,2048]{2,1,0:T(8,128)(2,1)S(1)} %broadcast_select_fusion.4.refs_12_), channel_id=1, source_target_pairs={{0,8},{8,16},{16,24},{24,28},{28,20},{20,12},{12,4},{4,0},{1,9},{9... | collective-permute-start | bytes 9437192 | tf_op jit(solution)/shard_map/ppermute | solution.py:385
  159.7 35.5 %collective-permute-start.22 = (bf16[768,2048]{1,0:T(8,128)(2,1)S(1)}, bf16[768,2048]{1,0:T(8,128)(2,1)}, u32[]{:S(2)}, u32[]{:S(2)}) collective-permute-start(bf16[768,2048]{1,0:T(8,128)(2,1)S(1)} %copy-done.6), channel_id=1, source_target_pairs={{1,2},{2,1},{5,6},{6,5},{9,10},{10,9},{13,14},{14,13},{17,18},{18,... | collective-permute-start | bytes 9437192 | tf_op jit(solution)/shard_map/ppermute | solution.py:376
  205.0 75.7 %collective-permute-start.23 = (bf16[3,256,2048]{2,1,0:T(8,128)(2,1)}, bf16[3,256,2048]{2,1,0:T(8,128)(2,1)}, u32[]{:S(2)}, u32[]{:S(2)}) collective-permute-start(bf16[3,256,2048]{2,1,0:T(8,128)(2,1)} %collective-permute-done.18.refs_13_), channel_id=1, source_target_pairs={{0,8},{8,16},{16,24},{24,28},{28,20},{20,12},{12,4},{4,0},{1,9},{9... | collective-permute-start | bytes 9437192 | tf_op jit(solution)/shard_map/ppermute | solution.py:385
  205.4 80.5 %collective-permute-start.24 = (bf16[3,256,2048]{2,1,0:T(8,128)(2,1)}, bf16[3,256,2048]{2,1,0:T(8,128)(2,1)}, u32[]{:S(2)}, u32[]{:S(2)}) collective-permute-start(bf16[3,256,2048]{2,1,0:T(8,128)(2,1)} %collective-permute-done.19.refs_14_), channel_id=1, source_target_pairs={{8,0},{16,8},{24,16},{28,24},{20,28},{12,20},{4,12},{0,4},{9,1},{1... | collective-permute-start | bytes 9437192 | tf_op jit(solution)/shard_map/ppermute | solution.py:385
  209.1 76.8 %collective-permute-start.29 = (bf16[768,2048]{1,0:T(8,128)(2,1)}, bf16[768,2048]{1,0:T(8,128)(2,1)}, u32[]{:S(2)}, u32[]{:S(2)}) collective-permute-start(bf16[768,2048]{1,0:T(8,128)(2,1)} %param.16), channel_id=1, source_target_pairs={{1,2},{2,1},{5,6},{6,5},{9,10},{10,9},{13,14},{14,13},{17,18},{18,... | collective-permute-start | bytes 9437192 | tf_op jit(solution)/shard_map/ppermute | solution.py:376
  229.5 56.4 %collective-permute-start.27 = (bf16[768,1024]{1,0:T(8,128)(2,1)}, bf16[768,1024]{1,0:T(8,128)(2,1)S(1)}, u32[]{:S(2)}, u32[]{:S(2)}) collective-permute-start(bf16[768,1024]{1,0:T(8,128)(2,1)} %forward_conv.2.refs_0_), channel_id=1, source_target_pairs={{0,1},{1,0},{2,3},{3,2},{4,5},{5,4},{6,7},{7,6},{8,9},{9,8},{10,11... | collective-permute-start | bytes 4718600 | tf_op jit(solution)/shard_map/ppermute | solution.py:382
  285.9 44.4 %collective-permute-start.34 = (bf16[768,1024]{1,0:T(8,128)(2,1)}, bf16[768,1024]{1,0:T(8,128)(2,1)}, u32[]{:S(2)}, u32[]{:S(2)}) collective-permute-start(bf16[768,1024]{1,0:T(8,128)(2,1)} %forward_conv.3.refs_1_), channel_id=1, source_target_pairs={{0,1},{1,0},{2,3},{3,2},{4,5},{5,4},{6,7},{7,6},{8,9},{9,8},{10,11... | collective-permute-start | bytes 4718600 | tf_op jit(solution)/shard_map/ppermute | solution.py:382
  289.9 38.2 %collective-permute-start.30 = (bf16[3,128,2048]{2,1,0:T(8,128)(2,1)S(1)}, bf16[3,128,2048]{2,1,0:T(8,128)(2,1)}, u32[]{:S(2)}, u32[]{:S(2)}) collective-permute-start(bf16[3,128,2048]{2,1,0:T(8,128)(2,1)S(1)} %get-tuple-element.180), channel_id=1, source_target_pairs={{0,8},{8,16},{16,24},{24,28},{28,20},{20,12},{12,4},{4,0},{1,9},{9... | collective-permute-start | bytes 4718600 | tf_op jit(solution)/shard_map/ppermute | solution.py:385
  293.3 36.4 %collective-permute-start.31 = (bf16[3,128,2048]{2,1,0:T(8,128)(2,1)S(1)}, bf16[3,128,2048]{2,1,0:T(8,128)(2,1)}, u32[]{:S(2)}, u32[]{:S(2)}) collective-permute-start(bf16[3,128,2048]{2,1,0:T(8,128)(2,1)S(1)} %get-tuple-element.178), channel_id=1, source_target_pairs={{8,0},{16,8},{24,16},{28,24},{20,28},{12,20},{4,12},{0,4},{9,1},{1... | collective-permute-start | bytes 4718600 | tf_op jit(solution)/shard_map/ppermute | solution.py:385
  330.3 37.4 %collective-permute-start.32 = (bf16[3,128,2048]{2,1,0:T(8,128)(2,1)}, bf16[3,128,2048]{2,1,0:T(8,128)(2,1)}, u32[]{:S(2)}, u32[]{:S(2)}) collective-permute-start(bf16[3,128,2048]{2,1,0:T(8,128)(2,1)} %get-tuple-element.179), channel_id=1, source_target_pairs={{0,8},{8,16},{16,24},{24,28},{28,20},{20,12},{12,4},{4,0},{1,9},{9... | collective-permute-start | bytes 4718600 | tf_op jit(solution)/shard_map/ppermute | solution.py:385
  333.1 36.3 %collective-permute-start.33 = (bf16[3,128,2048]{2,1,0:T(8,128)(2,1)}, bf16[3,128,2048]{2,1,0:T(8,128)(2,1)}, u32[]{:S(2)}, u32[]{:S(2)}) collective-permute-start(bf16[3,128,2048]{2,1,0:T(8,128)(2,1)} %get-tuple-element.177), channel_id=1, source_target_pairs={{8,0},{16,8},{24,16},{28,24},{20,28},{12,20},{4,12},{0,4},{9,1},{1... | collective-permute-start | bytes 4718600 | tf_op jit(solution)/shard_map/ppermute | solution.py:385
  369.4 47.8 %collective-permute-start.39 = (bf16[3,128,2048]{2,1,0:T(8,128)(2,1)}, bf16[3,128,2048]{2,1,0:T(8,128)(2,1)S(1)}, u32[]{:S(2)}, u32[]{:S(2)}) collective-permute-start(bf16[3,128,2048]{2,1,0:T(8,128)(2,1)} %collective-permute-done.30), channel_id=1, source_target_pairs={{0,8},{8,16},{16,24},{24,28},{28,20},{20,12},{12,4},{4,0},{1,9},{9... | collective-permute-start | bytes 4718600 | tf_op jit(solution)/shard_map/ppermute | solution.py:385
  371.1 46.1 %collective-permute-start.40 = (bf16[3,128,2048]{2,1,0:T(8,128)(2,1)}, bf16[3,128,2048]{2,1,0:T(8,128)(2,1)S(1)}, u32[]{:S(2)}, u32[]{:S(2)}) collective-permute-start(bf16[3,128,2048]{2,1,0:T(8,128)(2,1)} %collective-permute-done.33), channel_id=1, source_target_pairs={{8,0},{16,8},{24,16},{28,24},{20,28},{12,20},{4,12},{0,4},{9,1},{1... | collective-permute-start | bytes 4718600 | tf_op jit(solution)/shard_map/ppermute | solution.py:385
  371.6 45.6 %collective-permute-start.41 = (bf16[3,768,256]{2,1,0:T(8,128)(2,1)S(1)}, bf16[3,768,256]{2,1,0:T(8,128)(2,1)S(1)}, u32[]{:S(2)}, u32[]{:S(2)}) collective-permute-start(bf16[3,768,256]{2,1,0:T(8,128)(2,1)S(1)} %get-tuple-element.159), channel_id=1, source_target_pairs={{0,2},{2,0},{1,3},{3,1},{4,6},{6,4},{5,7},{7,5},{8,10},{10,8},{9,1... | collective-permute-start | bytes 3538952 | tf_op jit(solution)/shard_map/ppermute | solution.py:536
  390.0 27.2 %collective-permute-start.42 = (bf16[2,768,256]{2,1,0:T(8,128)(2,1)S(1)}, bf16[2,768,256]{2,1,0:T(8,128)(2,1)S(1)}, u32[]{:S(2)}, u32[]{:S(2)}) collective-permute-start(bf16[2,768,256]{2,1,0:T(8,128)(2,1)S(1)} %get-tuple-element.161), channel_id=1, source_target_pairs={{0,2},{2,0},{1,3},{3,1},{4,6},{6,4},{5,7},{7,5},{8,10},{10,8},{9,1... | collective-permute-start | bytes 2359304 | tf_op jit(solution)/shard_map/ppermute | solution.py:536
  417.4 30.6 %collective-permute-start.46 = (bf16[2,768,256]{2,1,0:T(8,128)(2,1)S(1)}, bf16[2,768,256]{2,1,0:T(8,128)(2,1)}, u32[]{:S(2)}, u32[]{:S(2)}) collective-permute-start(bf16[2,768,256]{2,1,0:T(8,128)(2,1)S(1)} %add_convert_fusion.2.refs_1_), channel_id=1, source_target_pairs={{0,1},{1,0},{2,3},{3,2},{4,5},{5,4},{6,7},{7,6},{8,9},{9,8},{10,11... | collective-permute-start | bytes 2359304 | tf_op jit(solution)/shard_map/ppermute | solution.py:382
  (39 other events, 837.1 us)
where the time goes:
time: 468 us; the launch traced here: 459 us
  Pallas kernels  161 us (34%)
  waiting for transfers between devices  128 us (27%)
  starting transfers between devices  98.9 us (21%)
  other arithmetic  48.9 us (10%)
  local copies, waits for them, and re-layouts  20.4 us (4%)
    ppermute x18, waiting for transfers between devices, both_ways(): return (lax.ppermute(up, ('o',), forth), lax.ppermute(down, ('o',), back))  81.3 us
    pallas_call x4, Pallas kernels, project(): pl.pallas_call(functools.partial(project_kernel, places, blocks), grid=(2...  70.8 us
    pallas_call x4, Pallas kernels, conv_call(): pl.pallas_call(functools.partial(kernel, taps, per), grid=(width // cols,...  56 us
    ppermute x13, starting transfers between devices, sibling(): return lax.ppermute(block, 'c', PAIR)  42.4 us
    ppermute x1, waiting for transfers between devices, on_device(): grad_other = lax.ppermute(grad_out, ('x', 'c'), CYCLE)  32.8 us
    pallas_call x1, Pallas kernels, mix_matmul(): pl.pallas_call(mix_kernel, grid_spec=pltpu.PrefetchScalarGridSpec(num_sca...  23.3 us
    ppermute x18, starting transfers between devices, both_ways(): return (lax.ppermute(up, ('o',), forth), lax.ppermute(down, ('o',), back))  20 us
    ppermute x3, starting transfers between devices, neighbour(): return lax.ppermute(block, ('o', 'x', 'c'), route)  16.1 us
  transfers between devices with their start and end apart: 49, of which 19 were waited for; matrix products, arithmetic and copies ran while one was open for 15% of the time, Pallas kernels for 33%

commit v1 on v0

--- a/solution.py
+++ b/solution.py
@@ -49,15 +49,20 @@
 
 
 def forward_kernel(
-    taps, count, base_ref, last_ref, tail_ref, keys_ref, values_ref, mix_ref, q_ref, table_ref, source_ref,
+    taps, count, own_ref, base_ref, last_ref, tail_ref, keys_ref, mix_ref, values_ref, other_values_ref,
+    q_ref, table_ref, source_ref,
 ):
     rows, width = keys_ref.shape
     parts = width // LANES
     toeplitz_into(table_ref, base_ref, taps, parts * count)
     source_ref[:taps, :] = tail_ref[...]
-    source_ref[taps:, :] = (keys_ref[...].astype(jnp.float32) * values_ref[...].astype(jnp.float32)).astype(
-        jnp.bfloat16
-    )
+    for flag, ref in ((1, values_ref), (0, other_values_ref)):
+
+        @pl.when(own_ref[0, 0] == flag)
+        def _(ref=ref):
+            source_ref[taps:, :] = (keys_ref[...].astype(jnp.float32) * ref[...].astype(jnp.float32)).astype(
+                jnp.bfloat16
+            )
 
     def tile(i, carry):
         row = pl.multiple_of(i * taps, taps)
@@ -75,14 +80,19 @@
 
 
 def backward_kernel(
-    taps, count, base_ref, last_ref, head_ref, keys_ref, values_ref, queries_ref, mix_ref,
-    k_ref, v_ref, table_ref, source_ref,
+    taps, count, own_ref, base_ref, last_ref, head_ref, keys_ref, mix_ref, values_ref, other_values_ref,
+    queries_ref, other_queries_ref, k_ref, v_ref, table_ref, source_ref, held_ref,
 ):
     rows, width = keys_ref.shape
     parts = width // LANES
     toeplitz_into(table_ref, base_ref, taps, parts * count)
-    source_ref[:rows, :] = (mix_ref[...] * queries_ref[...].astype(jnp.float32)).astype(jnp.bfloat16)
     source_ref[rows:, :] = head_ref[...]
+    for flag, values, queries in ((1, values_ref, queries_ref), (0, other_values_ref, other_queries_ref)):
+
+        @pl.when(own_ref[0, 0] == flag)
+        def _(values=values, queries=queries):
+            source_ref[:rows, :] = (mix_ref[...] * queries[...].astype(jnp.float32)).astype(jnp.bfloat16)
+            held_ref[...] = values[...]
 
     def tile(i, carry):
         row = pl.multiple_of(i * taps, taps)
@@ -93,14 +103,14 @@
             table = table_ref[p * count * taps : (p + 1) * count * taps, :]
             conv = banded(table, keep, source_ref[pl.ds(row, 2 * taps), lanes], taps, count)
             at = (pl.ds(row, taps), lanes)
-            k_ref[at] = (conv * values_ref[at].astype(jnp.float32)).astype(k_ref.dtype)
+            k_ref[at] = (conv * held_ref[at].astype(jnp.float32)).astype(k_ref.dtype)
             v_ref[at] = (conv * keys_ref[at].astype(jnp.float32)).astype(v_ref.dtype)
         return carry
 
     lax.fori_loop(0, rows // taps, tile, 0)
 
 
-def conv_call(kernel, name, base, last, edge, operands, outs, taps, per, width, start=0):
+def conv_call(kernel, name, own, base, last, edge, operands, outs, taps, per, width, start=0):
     rows = operands[0].shape[0]
     cols = min(width, 4 * LANES)
     count = cols // LANES * per
@@ -110,6 +120,7 @@
         functools.partial(kernel, taps, per),
         grid=(width // cols,),
         in_specs=[
+            pl.BlockSpec(memory_space=pltpu.SMEM),
             pl.BlockSpec((count, 2 * taps), lambda g: (g + skip, 0)),
             pl.BlockSpec(last.shape, lambda g: (0, 0)),
             pl.BlockSpec((taps, cols), lambda g: (0, g + skip)),
@@ -120,11 +131,12 @@
         scratch_shapes=[
             pltpu.VMEM((count * taps, 2 * taps), jnp.bfloat16),
             pltpu.VMEM((rows + taps, cols), jnp.bfloat16),
-        ],
+        ]
+        + [pltpu.VMEM((rows, cols), jnp.bfloat16)] * (outs - 1),
         compiler_params=params(1),
         cost_estimate=BRIEF,
         name=name,
-    )(base, last, edge, *operands)
+    )(own, base, last, edge, *operands)
 
 
 NT = (((1,), (1,)), ((), ()))
@@ -173,10 +185,27 @@
     )(at, *[grads] * len(lefts), own, sib)
 
 
-def project_kernel(places, blocks, *refs):
+def project_kernel(places, pieces, *refs):
     half = pl.num_programs(0) // 2
     own, sib = refs[: len(places)], refs[len(places) : 2 * len(places)]
-    weights, outs = refs[2 * len(places) : -2], refs[-2:]
+    parts, refs = refs[2 * len(places) : 2 * len(places) + sum(pieces)], refs[2 * len(places) + sum(pieces) :]
+    outs, joined = refs[:2], list(refs[2:])
+    blocks, weights, first = len(pieces), [], 0
+    for number in pieces:
+        block = parts[first : first + number]
+        first += number
+        if number == 1:
+            weights.append(block[0])
+            continue
+        whole = joined.pop(0)
+        weights.append(whole)
+
+        @pl.when(pl.program_id(0) == 0)
+        def _(block=block, whole=whole):
+            top = 0
+            for part in block:
+                whole[:, top : top + part.shape[1], :] = part[...]
+                top += part.shape[1]
 
     def into(grads, out_ref):
         for n in range(blocks):
@@ -197,8 +226,10 @@
 
 
 def project(own, sib, weights):
-    blocks = len(weights)
-    branches, feats, width = weights[0].shape
+    weights = [w if isinstance(w, tuple) else (w,) for w in weights]
+    blocks, pieces = len(weights), [len(w) for w in weights]
+    branches, _, width = weights[0][0].shape
+    feats = sum(part.shape[1] for part in weights[0])
     rows = own[0][0].shape[0]
     places = [
         (b, sum(p.shape[1] for p in pieces[:at])) for b, pieces in enumerate(own) for at in range(len(pieces))
@@ -215,23 +246,25 @@
 
     out = jax.ShapeDtypeStruct((blocks, rows, feats), jnp.bfloat16)
     return pl.pallas_call(
-        functools.partial(project_kernel, places, blocks),
+        functools.partial(project_kernel, places, pieces),
         grid=(2 * half,),
         in_specs=[pl.BlockSpec((step, p.shape[1]), lambda i: (first(i), 0)) for p in own]
         + [pl.BlockSpec((step, p.shape[1]), lambda i: (second(i), 0)) for p in sib]
         + [
-            pl.BlockSpec((branches, feats, width), lambda i: (0, 0, 0), pipeline_mode=pl.Buffered(1))
-        ]
-        * blocks,
+            pl.BlockSpec(part.shape, lambda i: (0, 0, 0), pipeline_mode=pl.Buffered(1))
+            for block in weights
+            for part in block
+        ],
         out_specs=[
             pl.BlockSpec((blocks, step, feats), lambda i: (0, first(i), 0)),
             pl.BlockSpec((blocks, step, feats), lambda i: (0, second(i), 0)),
         ],
         out_shape=[out, out],
+        scratch_shapes=[pltpu.VMEM((branches, feats, width), jnp.bfloat16)] * sum(n > 1 for n in pieces),
         compiler_params=params(1),
         cost_estimate=BRIEF,
         name="project",
-    )(*own, *sib, *weights)
+    )(*own, *sib, *[part for block in weights for part in block])
 
 
 def pick_kernel(at_ref, own_ref, sib_ref, input_ref, gain_ref, norm_ref, cross_ref):
@@ -493,7 +526,7 @@
     own_k = jnp.where(x == c, keys, k_recv)
     v_recv, values, own_k, queries, tail = fence(v_recv, values, own_k, queries, tail)
     q_recv = exchanged(queries)
-    own_v = jnp.where(x == c, values, v_recv)
+    ours = (x == c).astype(jnp.int32).reshape(1, 1)
     middle = width // 2
 
     def halves(kernel, name, *operands, outs):
@@ -502,7 +535,7 @@
         ]
 
     (q_left,), (q_right,) = halves(
-        forward_kernel, "forward_conv", base_fore, last_col, tail, [own_k, own_v, mix_grad], outs=1
+        forward_kernel, "forward_conv", ours, base_fore, last_col, tail, [own_k, mix_grad, values, v_recv], outs=1
     )
     sib_left = sibling(q_left)
     ahead[2], behind[2], q_left, q_right, sib_left, head, q_recv, queries = fence(
@@ -512,12 +545,11 @@
     upper, lower = slice(0, feats // 2), slice(feats // 2, feats)
     early = both_ways(ahead[2][:, upper], behind[2][:, upper])
     late = both_ways(ahead[2][:, lower], behind[2][:, lower])
-    own_q = jnp.where(x == c, queries, q_recv)
     grads = []
     for start in (0, middle):
         k_half, v_half = conv_call(
-            backward_kernel, "backward_conv", base_back, padded_last, head, [own_k, own_v, own_q, mix_grad], 2,
-            taps, per, middle, start,
+            backward_kernel, "backward_conv", ours, base_back, padded_last, head,
+            [own_k, mix_grad, values, v_recv, queries, q_recv], 2, taps, per, middle, start,
         )
         if start > 0:
             *early, k_half, v_half = fence(*early, k_half, v_half)
@@ -551,12 +583,14 @@
             keep, send, last_tail = fence(keep, send, own_grads[2][1])
             own_grads[2][1] = last_tail
             arrived.append((keep, over_x(send)))
-        keep, send = partial_sums([ahead[s - 1], behind[s - 1]])
+        keep, send = partial_sums(
+            [(early[0], late_up), (early[1], late_down)] if s == 4 else [ahead[s - 1], behind[s - 1]]
+        )
         flat = [block for pair in arrived for block in pair]
         up, down, keep, send, *flat = fence(up, down, keep, send, *flat)
         norms += [summed(*flat[i : i + 2]) for i in range(0, len(flat), 2)]
         ahead[s], behind[s] = up, down
-    far_keep, far_send = partial_sums([jnp.concatenate([up, down], axis=1)])
+    far_keep, far_send = partial_sums([(up, down)])
     norms += [summed(keep, over_x(send)), summed(far_keep, over_x(far_send))]
     slot = jnp.zeros((count,), jnp.int32).at[sources].set(jnp.arange(count, dtype=jnp.int32))
     if n_chan == 1:

time: 468 us -> 466 us (level)
  other arithmetic: 48.9 us -> 34 us
  starting transfers between devices: 98.9 us -> 107 us
    concatenate x3 -> x0, other arithmetic: 9.96 us -> none  [the longest x1 3.96 us: on_device(): ahead[3] = jnp.concatenate([early[0], late_up], axis=1)]
    select_n x2 -> x0, other arithmetic: 7.77 us -> none  [the longest x1 3.92 us: on_device(): own_q = jnp.where(x == c, queries, q_recv)]
    ppermute x13, starting transfers between devices: 42.4 us -> 47.9 us  [sibling(): return lax.ppermute(block, 'c', PAIR)]
    unnamed x35 -> x59, local copies, waits for them, and re-layouts: 7.44 us -> 9.8 us
  transfers between devices with their start and end apart: 49 -> 49, of which waited for: 19 -> 21; matrix products, arithmetic and copies ran while one was open for 15% -> 11% of each run, Pallas kernels for 33% -> 33%
where the time goes in v1:
time: 466 us; the launch traced here: 457 us
  Pallas kernels  161 us (35%)
  waiting for transfers between devices  129 us (28%)
  starting transfers between devices  107 us (23%)
  other arithmetic  34 us (7%)
  local copies, waits for them, and re-layouts  23.3 us (5%)
    ppermute x18, waiting for transfers between devices, both_ways(): return (lax.ppermute(up, ('o',), forth), lax.ppermute(down, ('o',), back))  78.7 us
    pallas_call x4, Pallas kernels, project(): pl.pallas_call(functools.partial(project_kernel, places, pieces), grid=(2...  71.2 us
    pallas_call x4, Pallas kernels, conv_call(): pl.pallas_call(functools.partial(kernel, taps, per), grid=(width // cols,...  55.8 us
    ppermute x13, starting transfers between devices, sibling(): return lax.ppermute(block, 'c', PAIR)  47.9 us
    ppermute x1, waiting for transfers between devices, on_device(): grad_other = lax.ppermute(grad_out, ('x', 'c'), CYCLE)  32.8 us
    pallas_call x1, Pallas kernels, mix_matmul(): pl.pallas_call(mix_kernel, grid_spec=pltpu.PrefetchScalarGridSpec(num_sca...  23.3 us
    ppermute x18, starting transfers between devices, both_ways(): return (lax.ppermute(up, ('o',), forth), lax.ppermute(down, ('o',), back))  21.3 us
    ppermute x3, starting transfers between devices, neighbour(): return lax.ppermute(block, ('o', 'x', 'c'), route)  17.6 us
  transfers between devices with their start and end apart: 49, of which 21 were waited for; matrix products, arithmetic and copies ran while one was open for 11% of the time, Pallas kernels for 33%

profile of v1, /device:TPU:0, one launch (start us, length us, event | category | flops | bytes accessed | tf_op | source)
XLA Modules:
  0.0 456.6 jit_solution(15327832992536445947)
XLA Ops:
  1.5 7.4 %collective-permute-start.3 = (s32[1,4]{1,0:T(1,128)}, s32[1,4]{1,0:T(1,128)S(1)}, u32[]{:S(2)}, u32[]{:S(2)}) collective-permute-start(s32[1,4]{1,0:T(1,128)} %param.20), channel_id=1, source_target_pairs={{0,1},{1,3},{2,4},{3,6},{4,5},{5,7},{6,8},{7,10},{8,9},{9,11},{10,... | collective-permute-start | bytes 56 | tf_op jit(solution)/shard_map/ppermute | solution.py:434
  32.2 19.2 %collective-permute-done.5 = bf16[2048,256]{1,0:T(8,128)(2,1)S(1)} collective-permute-done((bf16[2048,256]{1,0:T(8,128)(2,1)S(1)}, bf16[2048,256]{1,0:T(8,128)(2,1)S(1)}, u32[]{:S(2)}, u32[]{:S(2)}) %collective-permute-start.5) | collective-permute-done | bytes 1048608 | tf_op jit(solution)/shard_map/ppermute | solution.py:418
  56.1 19.5 %collective-permute-done.7 = bf16[2048,256]{1,0:T(8,128)(2,1)S(1)} collective-permute-done((bf16[2048,256]{1,0:T(8,128)(2,1)S(1)}, bf16[2048,256]{1,0:T(8,128)(2,1)S(1)}, u32[]{:S(2)}, u32[]{:S(2)}) %collective-permute-start.7) | collective-permute-done | bytes 1048608 | tf_op jit(solution)/shard_map/ppermute | solution.py:418
  82.8 8.4 %multiply_reduce_fusion = (f32[768]{0:T(1024)S(1)}, bf16[2,768,2048]{2,1,0:T(8,128)(2,1)}) fusion(bf16[1,768,2048]{2,1,0:T(8,128)(2,1)S(1)} %bitcast.37, bf16[1,768,2048]{2,1,0:T(8,128)(2,1)} %bitcast.18, pred[]{:T(512)S(6)} %eq.55), kind=kLoop, calls=%fused_computation.2 | loop fusion | flops 18873600 | bytes 12585985 | tf_op jit(solution)/shard_map/reduce_sum | solution.py:469
  105.6 8.3 %collective-permute-done.14 = bf16[1024,256]{1,0:T(8,128)(2,1)S(1)} collective-permute-done((bf16[1024,256]{1,0:T(8,128)(2,1)S(1)}, bf16[1024,256]{1,0:T(8,128)(2,1)S(1)}, u32[]{:S(2)}, u32[]{:S(2)}) %collective-permute-start.14) | collective-permute-done | bytes 524320 | tf_op jit(solution)/shard_map/ppermute | solution.py:418
  116.4 9.8 %collective-permute-start.21 = (bf16[8,2048,256]{2,1,0:T(8,128)(2,1)}, bf16[8,2048,256]{2,1,0:T(8,128)(2,1)}, u32[]{:S(2)}, u32[]{:S(2)}) collective-permute-start(bf16[8,2048,256]{2,1,0:T(8,128)(2,1)} %fusion.refs_4_), channel_id=1, source_target_pairs={{0,1},{1,0},{2,3},{3,2},{4,5},{5,4},{6,7},{7,6},{8,9},{9,8},{10,11... | collective-permute-start | bytes 25165832 | tf_op jit(solution)/shard_map/ppermute | solution.py:415
  129.9 32.8 %collective-permute-done.20 = bf16[768,2048]{1,0:T(8,128)(2,1)} collective-permute-done((bf16[768,2048]{1,0:T(8,128)(2,1)S(1)}, bf16[768,2048]{1,0:T(8,128)(2,1)}, u32[]{:S(2)}, u32[]{:S(2)}) %collective-permute-start.20) | collective-permute-done | bytes 3145760 | tf_op jit(solution)/shard_map/ppermute | solution.py:508
  165.3 5.3 %pad_maximum_fusion.refs_0_.refs_1_.refs_2_.refs_3_ = bf16[768,4096]{1,0:T(8,128)(2,1)} fusion(bf16[768,2048]{1,0:T(8,128)(2,1)} %collective-permute-done.20, bf16[768,2048]{1,0:T(8,128)(2,1)S(1)} %broadcast_select_fusion.1), kind=kLoop, calls=%fused_computation.4 | loop fusion | flops 12582912 | bytes 12582912 | tf_op jit(solution)/shard_map/concatenate | solution.py:516
  170.6 23.3 %mix_matmul.1.mix_ref = f32[768,2048]{1,0:T(8,128)} custom-call(s32[2,8]{1,0:T(2,128)S(1)} %pad_add_fusion.2.at_ref, bf16[768,4096]{1,0:T(8,128)(2,1)} %pad_maximum_fusion.refs_0_.refs_1_.refs_2_.refs_3_, bf16[768,4096]{1,0:T(8,128)(2,1)} %pad_maximum_fusion.refs_0_.refs_1_.refs_2_.refs_3_, ...), custom_call_target="tpu_custom_call" | custom-call | flops 1024 | bytes 1024 | tf_op jit(solution)/shard_map/mix_matmul/pallas_call | solution.py:173
  199.0 8.9 %collective-permute-start.26 = (bf16[128,2048]{1,0:T(8,128)(2,1)S(1)}, bf16[128,2048]{1,0:T(8,128)(2,1)S(1)}, u32[]{:S(2)}, u32[]{:S(2)}) collective-permute-start(bf16[128,2048]{1,0:T(8,128)(2,1)S(1)} %copy-done.18), channel_id=1, source_target_pairs={{0,1},{1,3},{2,4},{3,6},{4,5},{5,7},{6,8},{7,10},{8,9},{9,11},{10,... | collective-permute-start | bytes 1572872 | tf_op jit(solution)/shard_map/ppermute | solution.py:434
  218.0 13.9 %forward_conv.2.refs_0_ = bf16[768,1024]{1,0:T(8,128)(2,1)} custom-call(s32[1,1]{1,0:T(1,128)} %bitcast.20.own_ref, f32[128,256]{1,0:T(8,128)S(1)} %maximum_maximum_fusion.base_ref, s32[768,1]{1,0:T(8,128)S(1)} %copy.17.last_ref, bf16[128,2048]{1,0:T(8,128)(2,1)S(1)} %collective-permute-done.26.tail_ref, bf16[768,2048]{1,0:T(8,128)(2,1)} %broadcast_select_fusion.keys_ref, ...), custom_call_target="tpu_custom_call" | custom-call | flops 1024 | bytes 1024 | tf_op jit(solution)/shard_map/forward_conv/pallas_call | solution.py:119
  231.9 32.1 %collective-permute-start.27 = (bf16[768,1024]{1,0:T(8,128)(2,1)}, bf16[768,1024]{1,0:T(8,128)(2,1)S(1)}, u32[]{:S(2)}, u32[]{:S(2)}) collective-permute-start(bf16[768,1024]{1,0:T(8,128)(2,1)} %forward_conv.2.refs_0_), channel_id=1, source_target_pairs={{0,1},{1,0},{2,3},{3,2},{4,5},{5,4},{6,7},{7,6},{8,9},{9,8},{10,11... | collective-permute-start | bytes 4718600 | tf_op jit(solution)/shard_map/ppermute | solution.py:415
  267.0 13.8 %forward_conv.3.refs_1_ = bf16[768,1024]{1,0:T(8,128)(2,1)} custom-call(s32[1,1]{1,0:T(1,128)} %bitcast.20.own_ref, f32[128,256]{1,0:T(8,128)S(1)} %maximum_maximum_fusion.base_ref, s32[768,1]{1,0:T(8,128)S(1)} %copy.17.last_ref, bf16[128,2048]{1,0:T(8,128)(2,1)S(1)} %collective-permute-done.26.tail_ref, bf16[768,2048]{1,0:T(8,128)(2,1)} %broadcast_select_fusion.keys_ref, ...), custom_call_target="tpu_custom_call" | custom-call | flops 1024 | bytes 1024 | tf_op jit(solution)/shard_map/forward_conv/pallas_call | solution.py:119
  280.9 7.9 %collective-permute-done.24.refs_13_ = bf16[3,256,2048]{2,1,0:T(8,128)(2,1)} collective-permute-done((bf16[3,256,2048]{2,1,0:T(8,128)(2,1)}, bf16[3,256,2048]{2,1,0:T(8,128)(2,1)}, u32[]{:S(2)}, u32[]{:S(2)}) %collective-permute-start.24) | collective-permute-done | bytes 3145760 | tf_op jit(solution)/shard_map/ppermute | solution.py:418
  298.7 14.1 %backward_conv.3 = (bf16[768,1024]{1,0:T(8,128)(2,1)}, bf16[768,1024]{1,0:T(8,128)(2,1)}) custom-call(s32[1,1]{1,0:T(1,128)} %bitcast.20.own_ref, f32[128,256]{1,0:T(8,128)S(1)} %concatenate.31.base_ref, s32[1,896]{1,0:T(1,128)S(1)} %broadcast_in_dim.39.last_ref, bf16[128,2048]{1,0:T(8,128)(2,1)S(1)} %collective-permute-done.28.head_ref, ...), custom_call_target="tpu_custom_call" | custom-call | flops 1024 | bytes 1024 | tf_op jit(solution)/shard_map/backward_conv/pallas_call | solution.py:119
  313.3 14.0 %backward_conv.2 = (bf16[768,1024]{1,0:T(8,128)(2,1)}, bf16[768,1024]{1,0:T(8,128)(2,1)}) custom-call(s32[1,1]{1,0:T(1,128)} %bitcast.20.own_ref, f32[128,256]{1,0:T(8,128)S(1)} %concatenate.31.base_ref, s32[1,896]{1,0:T(1,128)S(1)} %broadcast_in_dim.39.last_ref, bf16[128,2048]{1,0:T(8,128)(2,1)S(1)} %collective-permute-done.28.head_ref, ...), custom_call_target="tpu_custom_call" | custom-call | flops 1024 | bytes 1024 | tf_op jit(solution)/shard_map/backward_conv/pallas_call | solution.py:119
  337.4 23.8 %project.4 = (bf16[3,768,256]{2,1,0:T(8,128)(2,1)S(1)}, bf16[3,768,256]{2,1,0:T(8,128)(2,1)}) custom-call(bf16[768,1024]{1,0:T(8,128)(2,1)} %forward_conv.2.refs_0_, bf16[768,1024]{1,0:T(8,128)(2,1)} %forward_conv.3.refs_1_, bf16[768,1024]{1,0:T(8,128)(2,1)} %get-tuple-element.142.refs_2_, bf16[768,1024]{1,0:T(8,128)(2,1)} %get-tuple-element.143.refs_3_, ...), custom_call_target="tpu_custom_call" | custom-call | flops 1024 | bytes 1024 | tf_op jit(solution)/shard_map/project/pallas_call | solution.py:248
  362.7 6.6 %collective-permute-done.32.refs_13_ = bf16[3,128,2048]{2,1,0:T(8,128)(2,1)} collective-permute-done((bf16[3,128,2048]{2,1,0:T(8,128)(2,1)}, bf16[3,128,2048]{2,1,0:T(8,128)(2,1)}, u32[]{:S(2)}, u32[]{:S(2)}) %collective-permute-start.32) | collective-permute-done | bytes 1572896 | tf_op jit(solution)/shard_map/ppermute | solution.py:418
  374.2 17.2 %project.5 = (bf16[2,768,256]{2,1,0:T(8,128)(2,1)S(1)}, bf16[2,768,256]{2,1,0:T(8,128)(2,1)S(1)}) custom-call(bf16[768,1024]{1,0:T(8,128)(2,1)} %forward_conv.2.refs_0_, bf16[768,1024]{1,0:T(8,128)(2,1)} %forward_conv.3.refs_1_, bf16[768,1024]{1,0:T(8,128)(2,1)} %get-tuple-element.142.refs_2_, bf16[768,1024]{1,0:T(8,128)(2,1)} %get-tuple-element.143.refs_3_, ...), custom_call_target="tpu_custom_call" | custom-call | flops 1024 | bytes 1024 | tf_op jit(solution)/shard_map/project/pallas_call | solution.py:248
  392.5 17.6 %project.6 = (bf16[2,768,256]{2,1,0:T(8,128)(2,1)S(1)}, bf16[2,768,256]{2,1,0:T(8,128)(2,1)S(1)}) custom-call(bf16[768,1024]{1,0:T(8,128)(2,1)} %forward_conv.2.refs_0_, bf16[768,1024]{1,0:T(8,128)(2,1)} %forward_conv.3.refs_1_, bf16[768,1024]{1,0:T(8,128)(2,1)} %get-tuple-element.142.refs_2_, bf16[768,1024]{1,0:T(8,128)(2,1)} %get-tuple-element.143.refs_3_, ...), custom_call_target="tpu_custom_call" | custom-call | flops 1024 | bytes 1024 | tf_op jit(solution)/shard_map/project/pallas_call | solution.py:248
  411.1 5.5 %collective-permute-done.42 = bf16[2,768,256]{2,1,0:T(8,128)(2,1)S(1)} collective-permute-done((bf16[2,768,256]{2,1,0:T(8,128)(2,1)}, bf16[2,768,256]{2,1,0:T(8,128)(2,1)S(1)}, u32[]{:S(2)}, u32[]{:S(2)}) %collective-permute-start.42) | collective-permute-done | bytes 786464 | tf_op jit(solution)/shard_map/ppermute | solution.py:568
  418.5 12.5 %project.7 = (bf16[1,768,256]{2,1,0:T(8,128)(2,1)S(1)}, bf16[1,768,256]{2,1,0:T(8,128)(2,1)S(1)}) custom-call(bf16[768,1024]{1,0:T(8,128)(2,1)} %forward_conv.2.refs_0_, bf16[768,1024]{1,0:T(8,128)(2,1)} %forward_conv.3.refs_1_, bf16[768,1024]{1,0:T(8,128)(2,1)} %get-tuple-element.142.refs_2_, bf16[768,1024]{1,0:T(8,128)(2,1)} %get-tuple-element.143.refs_3_, ...), custom_call_target="tpu_custom_call" | custom-call | flops 1024 | bytes 1024 | tf_op jit(solution)/shard_map/project/pallas_call | solution.py:248
  438.5 5.2 %collective-permute-done.44 = bf16[1,768,256]{2,1,0:T(8,128)(2,1)S(1)} collective-permute-done((bf16[1,768,256]{2,1,0:T(8,128)(2,1)S(1)}, bf16[1,768,256]{2,1,0:T(8,128)(2,1)S(1)}, u32[]{:S(2)}, u32[]{:S(2)}) %collective-permute-start.44) | collective-permute-done | bytes 393248 | tf_op jit(solution)/shard_map/ppermute | solution.py:568
  445.7 10.5 %finish.1 = bf16[768,2048]{1,0:T(8,128)(2,1)} custom-call(s32[3,8]{1,0:T(4,128)S(1)} %pad_add_fusion.1.at_ref, bf16[3,768,256]{2,1,0:T(8,128)(2,1)} %copy-done.8, bf16[2,768,256]{2,1,0:T(8,128)(2,1)S(1)} %add_convert_fusion.2.refs_1_, bf16[2,768,256]{2,1,0:T(8,128)(2,1)} %add_convert_fusion.1.refs_2_, bf16[1,768,256]{2,1,0:T(8,128)(2,1)S(1)} %add_convert_fusion.3.refs_3_, ...), custom_call_target="tpu_custom_call" | custom-call | flops 1024 | bytes 1024 | tf_op jit(solution)/shard_map/finish/pallas_call | solution.py:356
  (200 shorter events, 116.7 us)
Async XLA Ops:
  14.4 63.3 %collective-permute-start.10 = (bf16[768,2048]{1,0:T(8,128)(2,1)}, bf16[768,2048]{1,0:T(8,128)(2,1)}, u32[]{:S(2)}, u32[]{:S(2)}) collective-permute-start(bf16[768,2048]{1,0:T(8,128)(2,1)} %param.14), channel_id=1, source_target_pairs={{0,1},{1,0},{2,3},{3,2},{4,5},{5,4},{6,7},{7,6},{8,9},{9,8},{10,11... | collective-permute-start | bytes 9437192 | tf_op jit(solution)/shard_map/ppermute | solution.py:415
  19.0 37.0 %collective-permute-start.11 = (bf16[2048]{0:T(1024)(128)(2,1)}, bf16[2048]{0:T(1024)(128)(2,1)S(1)}, u32[]{:S(2)}, u32[]{:S(2)}) collective-permute-start(bf16[2048]{0:T(1024)(128)(2,1)} %param.15), channel_id=1, source_target_pairs={{0,1},{1,0},{2,3},{3,2},{4,5},{5,4},{6,7},{7,6},{8,9},{9,8},{10,11... | collective-permute-start | bytes 12296 | tf_op jit(solution)/shard_map/ppermute | solution.py:415
  21.8 55.9 %collective-permute-start.9 = (bf16[3,256,2048]{2,1,0:T(8,128)(2,1)}, bf16[3,256,2048]{2,1,0:T(8,128)(2,1)}, u32[]{:S(2)}, u32[]{:S(2)}) collective-permute-start(bf16[3,256,2048]{2,1,0:T(8,128)(2,1)} %bitcast.5), channel_id=1, source_target_pairs={{1,2},{2,1},{5,6},{6,5},{9,10},{10,9},{13,14},{14,13},{17,18},{18,... | collective-permute-start | bytes 9437192 | tf_op jit(solution)/shard_map/ppermute | solution.py:409
  25.6 25.8 %collective-permute-start.5 = (bf16[2048,256]{1,0:T(8,128)(2,1)S(1)}, bf16[2048,256]{1,0:T(8,128)(2,1)S(1)}, u32[]{:S(2)}, u32[]{:S(2)}) collective-permute-start(bf16[2048,256]{1,0:T(8,128)(2,1)S(1)} %broadcast_select_fusion.5), channel_id=1, source_target_pairs={{0,8},{8,16},{16,24},{24,28},{28,20},{20,12},{12,4},{4,0},{1,9},{9... | collective-permute-start | bytes 3145736 | tf_op jit(solution)/shard_map/ppermute | solution.py:418
  28.9 25.0 %collective-permute-start.6 = (bf16[2048,256]{1,0:T(8,128)(2,1)S(1)}, bf16[2048,256]{1,0:T(8,128)(2,1)S(1)}, u32[]{:S(2)}, u32[]{:S(2)}) collective-permute-start(bf16[2048,256]{1,0:T(8,128)(2,1)S(1)} %broadcast_select_fusion.5), channel_id=1, source_target_pairs={{8,0},{16,8},{24,16},{28,24},{20,28},{12,20},{4,12},{0,4},{9,1},{1... | collective-permute-start | bytes 3145736 | tf_op jit(solution)/shard_map/ppermute | solution.py:418
  51.4 24.2 %collective-permute-start.7 = (bf16[2048,256]{1,0:T(8,128)(2,1)S(1)}, bf16[2048,256]{1,0:T(8,128)(2,1)S(1)}, u32[]{:S(2)}, u32[]{:S(2)}) collective-permute-start(bf16[2048,256]{1,0:T(8,128)(2,1)S(1)} %collective-permute-done.5), channel_id=1, source_target_pairs={{0,8},{8,16},{16,24},{24,28},{28,20},{20,12},{12,4},{4,0},{1,9},{9... | collective-permute-start | bytes 3145736 | tf_op jit(solution)/shard_map/ppermute | solution.py:418
  81.9 34.5 %collective-permute-start.16 = (bf16[768,2048]{1,0:T(8,128)(2,1)S(1)}, bf16[768,2048]{1,0:T(8,128)(2,1)S(1)}, u32[]{:S(2)}, u32[]{:S(2)}) collective-permute-start(bf16[768,2048]{1,0:T(8,128)(2,1)S(1)} %copy-done.7), channel_id=1, source_target_pairs={{1,2},{2,1},{5,6},{6,5},{9,10},{10,9},{13,14},{14,13},{17,18},{18,... | collective-permute-start | bytes 9437192 | tf_op jit(solution)/shard_map/ppermute | solution.py:409
  116.4 54.2 %collective-permute-start.21 = (bf16[8,2048,256]{2,1,0:T(8,128)(2,1)}, bf16[8,2048,256]{2,1,0:T(8,128)(2,1)}, u32[]{:S(2)}, u32[]{:S(2)}) collective-permute-start(bf16[8,2048,256]{2,1,0:T(8,128)(2,1)} %fusion.refs_4_), channel_id=1, source_target_pairs={{0,1},{1,0},{2,3},{3,2},{4,5},{5,4},{6,7},{7,6},{8,9},{9,8},{10,11... | collective-permute-start | bytes 25165832 | tf_op jit(solution)/shard_map/ppermute | solution.py:415
  126.2 36.4 %collective-permute-start.20 = (bf16[768,2048]{1,0:T(8,128)(2,1)S(1)}, bf16[768,2048]{1,0:T(8,128)(2,1)}, u32[]{:S(2)}, u32[]{:S(2)}) collective-permute-start(bf16[768,2048]{1,0:T(8,128)(2,1)S(1)} %copy-done.7), channel_id=1, source_target_pairs={{0,2},{1,0},{2,3},{3,1},{4,6},{5,4},{6,7},{7,5},{8,10},{9,8},{10,1... | collective-permute-start | bytes 9437192 | tf_op jit(solution)/shard_map/ppermute | solution.py:508
  127.8 69.0 %collective-permute-start.18 = (bf16[3,256,2048]{2,1,0:T(8,128)(2,1)S(1)}, bf16[3,256,2048]{2,1,0:T(8,128)(2,1)}, u32[]{:S(2)}, u32[]{:S(2)}) collective-permute-start(bf16[3,256,2048]{2,1,0:T(8,128)(2,1)S(1)} %broadcast_select_fusion.2.refs_12_), channel_id=1, source_target_pairs={{0,8},{8,16},{16,24},{24,28},{28,20},{20,12},{12,4},{4,0},{1,9},{9... | collective-permute-start | bytes 9437192 | tf_op jit(solution)/shard_map/ppermute | solution.py:418
  129.4 68.7 %collective-permute-start.19 = (bf16[3,256,2048]{2,1,0:T(8,128)(2,1)S(1)}, bf16[3,256,2048]{2,1,0:T(8,128)(2,1)}, u32[]{:S(2)}, u32[]{:S(2)}) collective-permute-start(bf16[3,256,2048]{2,1,0:T(8,128)(2,1)S(1)} %broadcast_select_fusion.2.refs_12_), channel_id=1, source_target_pairs={{8,0},{16,8},{24,16},{28,24},{20,28},{12,20},{4,12},{0,4},{9,1},{1... | collective-permute-start | bytes 9437192 | tf_op jit(solution)/shard_map/ppermute | solution.py:418
  162.6 35.5 %collective-permute-start.22 = (bf16[768,2048]{1,0:T(8,128)(2,1)S(1)}, bf16[768,2048]{1,0:T(8,128)(2,1)}, u32[]{:S(2)}, u32[]{:S(2)}) collective-permute-start(bf16[768,2048]{1,0:T(8,128)(2,1)S(1)} %copy-done.9), channel_id=1, source_target_pairs={{1,2},{2,1},{5,6},{6,5},{9,10},{10,9},{13,14},{14,13},{17,18},{18,... | collective-permute-start | bytes 9437192 | tf_op jit(solution)/shard_map/ppermute | solution.py:409
  207.9 73.0 %collective-permute-start.23 = (bf16[3,256,2048]{2,1,0:T(8,128)(2,1)}, bf16[3,256,2048]{2,1,0:T(8,128)(2,1)}, u32[]{:S(2)}, u32[]{:S(2)}) collective-permute-start(bf16[3,256,2048]{2,1,0:T(8,128)(2,1)} %collective-permute-done.18.refs_13_), channel_id=1, source_target_pairs={{0,8},{8,16},{16,24},{24,28},{28,20},{20,12},{12,4},{4,0},{1,9},{9... | collective-permute-start | bytes 9437192 | tf_op jit(solution)/shard_map/ppermute | solution.py:418
  209.5 79.3 %collective-permute-start.24 = (bf16[3,256,2048]{2,1,0:T(8,128)(2,1)}, bf16[3,256,2048]{2,1,0:T(8,128)(2,1)}, u32[]{:S(2)}, u32[]{:S(2)}) collective-permute-start(bf16[3,256,2048]{2,1,0:T(8,128)(2,1)} %collective-permute-done.19.refs_14_), channel_id=1, source_target_pairs={{8,0},{16,8},{24,16},{28,24},{20,28},{12,20},{4,12},{0,4},{9,1},{1... | collective-permute-start | bytes 9437192 | tf_op jit(solution)/shard_map/ppermute | solution.py:418
  215.5 73.3 %collective-permute-start.29 = (bf16[768,2048]{1,0:T(8,128)(2,1)}, bf16[768,2048]{1,0:T(8,128)(2,1)}, u32[]{:S(2)}, u32[]{:S(2)}) collective-permute-start(bf16[768,2048]{1,0:T(8,128)(2,1)} %queries_ref.1), channel_id=1, source_target_pairs={{1,2},{2,1},{5,6},{6,5},{9,10},{10,9},{13,14},{14,13},{17,18},{18,... | collective-permute-start | bytes 9437192 | tf_op jit(solution)/shard_map/ppermute | solution.py:409
  231.9 56.8 %collective-permute-start.27 = (bf16[768,1024]{1,0:T(8,128)(2,1)}, bf16[768,1024]{1,0:T(8,128)(2,1)S(1)}, u32[]{:S(2)}, u32[]{:S(2)}) collective-permute-start(bf16[768,1024]{1,0:T(8,128)(2,1)} %forward_conv.2.refs_0_), channel_id=1, source_target_pairs={{0,1},{1,0},{2,3},{3,2},{4,5},{5,4},{6,7},{7,6},{8,9},{9,8},{10,11... | collective-permute-start | bytes 4718600 | tf_op jit(solution)/shard_map/ppermute | solution.py:415
  292.8 35.9 %collective-permute-start.30 = (bf16[3,128,2048]{2,1,0:T(8,128)(2,1)S(1)}, bf16[3,128,2048]{2,1,0:T(8,128)(2,1)S(1)}, u32[]{:S(2)}, u32[]{:S(2)}) collective-permute-start(bf16[3,128,2048]{2,1,0:T(8,128)(2,1)S(1)} %get-tuple-element.180), channel_id=1, source_target_pairs={{0,8},{8,16},{16,24},{24,28},{28,20},{20,12},{12,4},{4,0},{1,9},{9... | collective-permute-start | bytes 4718600 | tf_op jit(solution)/shard_map/ppermute | solution.py:418
  296.2 35.1 %collective-permute-start.31 = (bf16[3,128,2048]{2,1,0:T(8,128)(2,1)S(1)}, bf16[3,128,2048]{2,1,0:T(8,128)(2,1)S(1)}, u32[]{:S(2)}, u32[]{:S(2)}) collective-permute-start(bf16[3,128,2048]{2,1,0:T(8,128)(2,1)S(1)} %get-tuple-element.178), channel_id=1, source_target_pairs={{8,0},{16,8},{24,16},{28,24},{20,28},{12,20},{4,12},{0,4},{9,1},{1... | collective-permute-start | bytes 4718600 | tf_op jit(solution)/shard_map/ppermute | solution.py:418
  332.5 36.8 %collective-permute-start.32 = (bf16[3,128,2048]{2,1,0:T(8,128)(2,1)}, bf16[3,128,2048]{2,1,0:T(8,128)(2,1)}, u32[]{:S(2)}, u32[]{:S(2)}) collective-permute-start(bf16[3,128,2048]{2,1,0:T(8,128)(2,1)} %get-tuple-element.179), channel_id=1, source_target_pairs={{0,8},{8,16},{16,24},{24,28},{28,20},{20,12},{12,4},{4,0},{1,9},{9... | collective-permute-start | bytes 4718600 | tf_op jit(solution)/shard_map/ppermute | solution.py:418
  332.5 36.9 %collective-permute-start.33 = (bf16[3,128,2048]{2,1,0:T(8,128)(2,1)}, bf16[3,128,2048]{2,1,0:T(8,128)(2,1)}, u32[]{:S(2)}, u32[]{:S(2)}) collective-permute-start(bf16[3,128,2048]{2,1,0:T(8,128)(2,1)} %get-tuple-element.177), channel_id=1, source_target_pairs={{8,0},{16,8},{24,16},{28,24},{20,28},{12,20},{4,12},{0,4},{9,1},{1... | collective-permute-start | bytes 4718600 | tf_op jit(solution)/shard_map/ppermute | solution.py:418
  369.5 47.2 %collective-permute-start.39 = (bf16[3,128,2048]{2,1,0:T(8,128)(2,1)S(1)}, bf16[3,128,2048]{2,1,0:T(8,128)(2,1)S(1)}, u32[]{:S(2)}, u32[]{:S(2)}) collective-permute-start(bf16[3,128,2048]{2,1,0:T(8,128)(2,1)S(1)} %copy-done.12), channel_id=1, source_target_pairs={{0,8},{8,16},{16,24},{24,28},{28,20},{20,12},{12,4},{4,0},{1,9},{9... | collective-permute-start | bytes 4718600 | tf_op jit(solution)/shard_map/ppermute | solution.py:418
  371.2 45.4 %collective-permute-start.40 = (bf16[3,128,2048]{2,1,0:T(8,128)(2,1)}, bf16[3,128,2048]{2,1,0:T(8,128)(2,1)S(1)}, u32[]{:S(2)}, u32[]{:S(2)}) collective-permute-start(bf16[3,128,2048]{2,1,0:T(8,128)(2,1)} %collective-permute-done.33.refs_15_), channel_id=1, source_target_pairs={{8,0},{16,8},{24,16},{28,24},{20,28},{12,20},{4,12},{0,4},{9,1},{1... | collective-permute-start | bytes 4718600 | tf_op jit(solution)/shard_map/ppermute | solution.py:418
  371.7 45.0 %collective-permute-start.41 = (bf16[3,768,256]{2,1,0:T(8,128)(2,1)S(1)}, bf16[3,768,256]{2,1,0:T(8,128)(2,1)S(1)}, u32[]{:S(2)}, u32[]{:S(2)}) collective-permute-start(bf16[3,768,256]{2,1,0:T(8,128)(2,1)S(1)} %get-tuple-element.159), channel_id=1, source_target_pairs={{0,2},{2,0},{1,3},{3,1},{4,6},{6,4},{5,7},{7,5},{8,10},{10,8},{9,1... | collective-permute-start | bytes 3538952 | tf_op jit(solution)/shard_map/ppermute | solution.py:568
  392.5 24.2 %collective-permute-start.42 = (bf16[2,768,256]{2,1,0:T(8,128)(2,1)}, bf16[2,768,256]{2,1,0:T(8,128)(2,1)S(1)}, u32[]{:S(2)}, u32[]{:S(2)}) collective-permute-start(bf16[2,768,256]{2,1,0:T(8,128)(2,1)} %get-tuple-element.161), channel_id=1, source_target_pairs={{0,2},{2,0},{1,3},{3,1},{4,6},{6,4},{5,7},{7,5},{8,10},{10,8},{9,1... | collective-permute-start | bytes 2359304 | tf_op jit(solution)/shard_map/ppermute | solution.py:568
  (51 other events, 855.9 us)
